TPU v7x, 32 devices: a whole 2x2x4 slice. The times are simulated.
32 devices in a mesh: tm: 8 (over z, x), chan: 4 (over y, core).
Axes of the slice: x: 2, y: 2, z: 4, core: 2. Of those that a mesh axis runs over, the one named last changes fastest.
Arguments:
- inner_x: bfloat16 [512, 1152], P('tm', 'chan'), may hold values from -6 to 6
- gate_z: bfloat16 [512, 1152], P('tm', 'chan'), may hold values from -6 to 6
- dt_raw: bfloat16 [512, 1152], P('tm', 'chan'), may hold values from -3 to 3
- grad_out: bfloat16 [512, 1152], P('tm', 'chan'), may hold values from -6 to 6
- input_b: bfloat16 [512, 16], P('tm'), may hold values from -1.5 to 1.5
- output_c: bfloat16 [512, 16], P('tm'), may hold values from -1.5 to 1.5
- conv_weight: float32 [4, 1152], P(None, 'chan'), may hold values from -3 to 3
- conv_bias: float32 [1152], P('chan'), may hold values from -0.5 to 0.5
- decay_log: float32 [16, 1152], P(None, 'chan'), as said below
- skip_gain: float32 [1152], P('chan'), may hold values from 0.5 to 1.5
Outputs:
- grad_x: bfloat16 [512, 1152], P('tm', 'chan')
- grad_dt: bfloat16 [512, 1152], P('tm', 'chan')
- grad_z: bfloat16 [512, 1152], P('tm', 'chan')
- grad_b: bfloat16 [512, 16], P('tm')
- grad_c: bfloat16 [512, 16], P('tm')
Inputs may be any that keep to these rules, and one draw needn't show every extreme that they name: `decay_log`: each entry is the natural logarithm of a positive decay rate.
All inputs are finite; a program needn't handle non-finite values.
Results may differ from a plain program's by a relative error of at most 0.0085.
Values may be sent and summed in bfloat16 or wider, within the bound.
A program may use at most 64 MiB of HBM per device.

v0:
```python
import math

import jax
import jax.numpy as jnp
from jax import lax
from jax.sharding import PartitionSpec as P

S_DEV = 2


def from_behind(value, axis, steps):
    count = lax.axis_size(axis)
    initial, last = (max(0, -steps), min(count, count - steps))
    return lax.ppermute(value, axis, [(source, source + steps) for source in range(initial, last)])


def entering(part, axis, combine, identity, reverse):
    count = lax.axis_size(axis)
    place = lax.axis_index(axis)
    ahead = count - 1 - place if reverse else place
    gathered = jax.tree.map(lambda a: lax.all_gather(a, axis), part)
    state = jax.tree.map(lambda a, e: jnp.zeros_like(a) + jnp.asarray(e, a.dtype), part, identity)

    def one(turn, state):
        source = count - 1 - turn if reverse else turn
        return combine(
            state, jax.tree.map(lambda a: lax.dynamic_index_in_dim(a, source, 0, False), gathered)
        )

    return lax.fori_loop(0, ahead, one, state)


def silu_grad(values):
    sigm = jax.nn.sigmoid(values)
    return sigm * (1.0 + values * (1.0 - sigm))


def combine(earlier, later):
    return (earlier[0] * later[0], earlier[1] * later[0] + later[1])


def on_device(
    inner_x,
    gate_z,
    dt_raw,
    grad_out,
    input_b,
    output_c,
    conv_weight,
    conv_bias,
    decay_log,
    skip_gain,
):
    tm_count = lax.axis_size("tm")
    row_count = inner_x.shape[0]
    spatial = S_DEV * tm_count
    frames = row_count // spatial
    conv_len = conv_weight.shape[0]

    def to_frames(array):
        return array.reshape(frames, spatial, array.shape[-1])

    def to_seq(array):
        return jnp.swapaxes(array, 0, 1).reshape(-1, array.shape[-1])

    def from_seq(array):
        return jnp.swapaxes(array.reshape(S_DEV, frames * tm_count, array.shape[-1]), 0, 1)

    def to_rows(array):
        return array.reshape(row_count, array.shape[-1])

    arrived = (
        lax.all_to_all(to_frames(inner_x), "tm", split_axis=1, concat_axis=0, tiled=True),
        lax.all_to_all(to_frames(dt_raw), "tm", split_axis=1, concat_axis=0, tiled=True),
        lax.all_to_all(to_frames(gate_z), "tm", split_axis=1, concat_axis=0, tiled=True),
        lax.all_to_all(to_frames(grad_out), "tm", split_axis=1, concat_axis=0, tiled=True),
        lax.all_to_all(to_frames(input_b), "tm", split_axis=1, concat_axis=0, tiled=True),
        lax.all_to_all(to_frames(output_c), "tm", split_axis=1, concat_axis=0, tiled=True),
    )
    seq_x, seq_dt, seq_z, seq_grad, seq_b, seq_c = [to_seq(member) for member in arrived]
    seq_dy = (seq_grad.astype(jnp.float32) * jax.nn.silu(seq_z.astype(jnp.float32))).astype(
        jnp.bfloat16
    )
    length = seq_x.shape[0]
    block_len = math.gcd(length, 32)
    blocks = length // block_len
    dt_vals = seq_dt.astype(jnp.float32)
    deltas = jax.nn.softplus(dt_vals)
    rim_rows = from_behind(seq_x[length - conv_len + 1 :], "tm", 1)
    padded = jnp.concatenate([rim_rows, seq_x]).astype(jnp.float32)
    pre_act = conv_bias[None, :] + conv_weight[0][None, :] * padded[0:length]
    for offset in range(1, conv_len):
        pre_act = pre_act + conv_weight[offset][None, :] * padded[offset : offset + length]
    conv_out = jax.nn.silu(pre_act)
    decay_rate = -jnp.exp(decay_log)
    b_vals = seq_b.astype(jnp.float32)
    c_vals = seq_c.astype(jnp.float32)
    dy_vals = seq_dy.astype(jnp.float32)

    def blocked(array):
        return array.reshape(blocks, block_len, array.shape[-1])

    def forward_block(state, items):
        delta_blk, conv_blk, b_blk = items
        start_state = state
        for offset in range(block_len):
            state = (
                jnp.exp(delta_blk[offset][None, :] * decay_rate) * state
                + (delta_blk[offset] * conv_blk[offset])[None, :] * b_blk[offset][:, None]
            )
        return (state, start_state)

    zero_state = jnp.zeros(decay_rate.shape, jnp.float32)
    local_end, local_starts = lax.scan(
        forward_block, zero_state, (blocked(deltas), blocked(conv_out), blocked(b_vals))
    )

    def adjoint_block(carry, items):
        delta_blk, c_blk, dy_blk = items
        for offset in reversed(range(block_len)):
            adjoint = c_blk[offset][:, None] * dy_blk[offset][None, :] + carry
            carry = jnp.exp(delta_blk[offset][None, :] * decay_rate) * adjoint
        return (carry, None)

    local_adjoint = lax.scan(
        adjoint_block,
        zero_state,
        (blocked(deltas), blocked(c_vals), blocked(dy_vals)),
        reverse=True,
    )[0]
    through = jnp.exp(decay_rate * jnp.sum(deltas, axis=0)[None, :])
    unit_pair = (jnp.ones_like(zero_state), zero_state)
    state_in = entering((through, local_end), "tm", combine, unit_pair, False)[1]
    adjoint_in = entering((through, local_adjoint), "tm", combine, unit_pair, True)[1]
    block_sums = jnp.sum(blocked(deltas), axis=1)
    before = jnp.concatenate(
        [jnp.zeros((1, block_sums.shape[1]), jnp.float32), jnp.cumsum(block_sums, axis=0)[:-1]]
    )
    full_starts = local_starts + jnp.exp(decay_rate[None] * before[:, None, :]) * state_in[None]

    def backward_block(carry, items):
        start_state, delta_blk, conv_blk, b_blk, c_blk, dy_blk = items
        state = start_state
        previous = []
        decays = []
        current = []
        for offset in range(block_len):
            decay_now = jnp.exp(delta_blk[offset][None, :] * decay_rate)
            previous.append(state)
            state = (
                decay_now * state
                + (delta_blk[offset] * conv_blk[offset])[None, :] * b_blk[offset][:, None]
            )
            decays.append(decay_now)
            current.append(state)
        y_rows = []
        conv_rows = []
        delta_rows = []
        b_rows = []
        c_rows = []
        for offset in reversed(range(block_len)):
            adjoint = c_blk[offset][:, None] * dy_blk[offset][None, :] + carry
            y_rows.append(
                jnp.sum(c_blk[offset][:, None] * current[offset], axis=0)
                + skip_gain * conv_blk[offset]
            )
            c_rows.append(jnp.sum(dy_blk[offset][None, :] * current[offset], axis=1))
            weighted = jnp.sum(adjoint * b_blk[offset][:, None], axis=0)
            conv_rows.append(skip_gain * dy_blk[offset] + delta_blk[offset] * weighted)
            b_rows.append(
                jnp.sum(adjoint * (delta_blk[offset] * conv_blk[offset])[None, :], axis=1)
            )
            delta_rows.append(
                jnp.sum(adjoint * decay_rate * decays[offset] * previous[offset], axis=0)
                + conv_blk[offset] * weighted
            )
            carry = decays[offset] * adjoint
        stacked = tuple(
            (
                jnp.stack(rows_list[::-1])
                for rows_list in (y_rows, conv_rows, delta_rows, b_rows, c_rows)
            )
        )
        return (carry, stacked)

    outputs = lax.scan(
        backward_block,
        adjoint_in,
        (
            full_starts,
            blocked(deltas),
            blocked(conv_out),
            blocked(b_vals),
            blocked(c_vals),
            blocked(dy_vals),
        ),
        reverse=True,
    )[1]
    y_full, grad_conv, grad_delta, part_b, part_c = [
        member.reshape(length, member.shape[-1]) for member in outputs
    ]
    seq_y = y_full.astype(jnp.bfloat16)
    grad_pre = grad_conv * silu_grad(pre_act)
    back_rows = from_behind(grad_pre[: conv_len - 1], "tm", -1)
    extended = jnp.concatenate([grad_pre, back_rows])
    grad_sx = conv_weight[0][None, :] * extended[conv_len - 1 : conv_len - 1 + length]
    for offset in range(1, conv_len):
        start_row = conv_len - 1 - offset
        grad_sx = grad_sx + conv_weight[offset][None, :] * extended[start_row : start_row + length]
    grad_sx = grad_sx.astype(jnp.bfloat16)
    grad_sdt = (grad_delta * jax.nn.sigmoid(dt_vals)).astype(jnp.bfloat16)
    sums_b, sums_c = lax.psum((part_b, part_c), "chan")
    grad_sb = sums_b.astype(jnp.bfloat16)
    grad_sc = sums_c.astype(jnp.bfloat16)
    grad_sz = (
        seq_grad.astype(jnp.float32)
        * seq_y.astype(jnp.float32)
        * silu_grad(seq_z.astype(jnp.float32))
    ).astype(jnp.bfloat16)
    returned = (
        lax.all_to_all(from_seq(grad_sx), "tm", split_axis=0, concat_axis=1, tiled=True),
        lax.all_to_all(from_seq(grad_sdt), "tm", split_axis=0, concat_axis=1, tiled=True),
        lax.all_to_all(from_seq(grad_sz), "tm", split_axis=0, concat_axis=1, tiled=True),
        lax.all_to_all(from_seq(grad_sb), "tm", split_axis=0, concat_axis=1, tiled=True),
        lax.all_to_all(from_seq(grad_sc), "tm", split_axis=0, concat_axis=1, tiled=True),
    )
    grad_x, grad_dt, grad_z, grad_b, grad_c = [to_rows(member) for member in returned]
    return (grad_x, grad_dt, grad_z, grad_b, grad_c)


def solution(mesh):
    return jax.shard_map(
        on_device,
        mesh=mesh,
        in_specs=(
            P("tm", "chan"),
            P("tm", "chan"),
            P("tm", "chan"),
            P("tm", "chan"),
            P("tm", None),
            P("tm", None),
            P(None, "chan"),
            P("chan"),
            P(None, "chan"),
            P("chan"),
        ),
        out_specs=(P("tm", "chan"), P("tm", "chan"), P("tm", "chan"), P("tm", None), P("tm", None)),
        check_vma=False,
    )
```

profile of v0, /device:TPU:0, one launch (start us, length us, event | category | flops | bytes accessed | tf_op | source)
XLA Modules:
  0.0 244.7 jit_solution(14177440652352672676)
XLA Ops:
  2.1 7.4 %all-to-all-start.5 = ((bf16[4,16,16]{2,0,1:T(4,128)(2,1)}), bf16[4,16,16]{2,0,1:T(4,128)(2,1)S(1)}, u32[]{:S(2)}, u32[]{:S(2)}) async-start(bf16[4,16,16]{2,0,1:T(4,128)(2,1)} %copy.173), calls=%async_computation.5 | async-start | bytes 32768 | tf_op jit(solution)/shard_map/all_to_all | solution.py:77
  10.3 5.8 %all-to-all-done.5 = bf16[4,16,16]{2,0,1:T(4,128)(2,1)S(1)} async-done(((bf16[4,16,16]{2,0,1:T(4,128)(2,1)}), bf16[4,16,16]{2,0,1:T(4,128)(2,1)S(1)}, u32[]{:S(2)}, u32[]{:S(2)}) %all-to-all-start.5) | async-done | bytes 2080 | tf_op jit(solution)/shard_map/all_to_all | solution.py:77
  22.5 3.4 %all-to-all-done.1 = bf16[4,16,16]{2,0,1:T(4,128)(2,1)S(1)} async-done(((bf16[4,16,16]{2,0,1:T(4,128)(2,1)}), bf16[4,16,16]{2,0,1:T(4,128)(2,1)S(1)}, u32[]{:S(2)}, u32[]{:S(2)}) %all-to-all-start.1) | async-done | bytes 2080 | tf_op jit(solution)/shard_map/all_to_all | solution.py:78
  25.9 3.3 %all-to-all-start.4 = ((bf16[4,16,288]{2,0,1:T(4,128)(2,1)}), bf16[4,16,288]{2,0,1:T(4,128)(2,1)S(1)}, u32[]{:S(2)}, u32[]{:S(2)}) async-start(bf16[4,16,288]{2,0,1:T(4,128)(2,1)} %copy.171), calls=%async_computation.4 | async-start | bytes 98304 | tf_op jit(solution)/shard_map/all_to_all | solution.py:73
  29.3 6.7 %all-to-all-done.4 = bf16[4,16,288]{2,0,1:T(4,128)(2,1)S(1)} async-done(((bf16[4,16,288]{2,0,1:T(4,128)(2,1)}), bf16[4,16,288]{2,0,1:T(4,128)(2,1)S(1)}, u32[]{:S(2)}, u32[]{:S(2)}) %all-to-all-start.4) | async-done | bytes 36896 | tf_op jit(solution)/shard_map/all_to_all | solution.py:73
  36.0 3.3 %all-to-all-start.3 = ((bf16[4,16,288]{2,0,1:T(4,128)(2,1)}), bf16[4,16,288]{2,0,1:T(4,128)(2,1)S(1)}, u32[]{:S(2)}, u32[]{:S(2)}) async-start(bf16[4,16,288]{2,0,1:T(4,128)(2,1)} %copy.168), calls=%async_computation.3 | async-start | bytes 98304 | tf_op jit(solution)/shard_map/all_to_all | solution.py:75
  39.5 3.8 %collective-permute-start = (bf16[3,288]{1,0:T(4,128)(2,1)S(1)}, bf16[3,288]{1,0:T(4,128)(2,1)S(1)}, u32[]{:S(2)}, u32[]{:S(2)}) collective-permute-start(bf16[3,288]{1,0:T(4,128)(2,1)S(1)} %slice.3548), channel_id=1, source_target_pairs={{0,4},{4,8},{8,12},{12,16},{16,20},{20,24},{24,28},{1,5},{5,9},{9,... | collective-permute-start | bytes 5192 | tf_op jit(solution)/shard_map/ppermute | solution.py:14
  46.1 3.3 %all-to-all-start = ((bf16[4,16,288]{2,0,1:T(4,128)(2,1)}), bf16[4,16,288]{2,0,1:T(4,128)(2,1)S(1)}, u32[]{:S(2)}, u32[]{:S(2)}) async-start(bf16[4,16,288]{2,0,1:T(4,128)(2,1)} %copy.159), calls=%async_computation | async-start | bytes 98304 | tf_op jit(solution)/shard_map/all_to_all | solution.py:74
  49.5 6.7 %all-to-all-done = bf16[4,16,288]{2,0,1:T(4,128)(2,1)S(1)} async-done(((bf16[4,16,288]{2,0,1:T(4,128)(2,1)}), bf16[4,16,288]{2,0,1:T(4,128)(2,1)S(1)}, u32[]{:S(2)}, u32[]{:S(2)}) %all-to-all-start) | async-done | bytes 36896 | tf_op jit(solution)/shard_map/all_to_all | solution.py:74
  56.2 3.3 %all-to-all-start.2 = ((bf16[4,16,288]{2,0,1:T(4,128)(2,1)}), bf16[4,16,288]{2,0,1:T(4,128)(2,1)S(1)}, u32[]{:S(2)}, u32[]{:S(2)}) async-start(bf16[4,16,288]{2,0,1:T(4,128)(2,1)} %copy.165), calls=%async_computation.2 | async-start | bytes 98304 | tf_op jit(solution)/shard_map/all_to_all | solution.py:76
  59.7 6.6 %all-to-all-done.2 = bf16[4,16,288]{2,0,1:T(4,128)(2,1)S(1)} async-done(((bf16[4,16,288]{2,0,1:T(4,128)(2,1)}), bf16[4,16,288]{2,0,1:T(4,128)(2,1)S(1)}, u32[]{:S(2)}, u32[]{:S(2)}) %all-to-all-start.2) | async-done | bytes 36896 | tf_op jit(solution)/shard_map/all_to_all | solution.py:76
  69.6 30.6 %all-gather.1 = f32[128,288]{1,0:T(8,128)S(1)} all-gather(f32[16,288]{1,0:T(8,128)S(1)} %get-tuple-element.590), channel_id=3, replica_groups=mesh['tm'=8,'chan'=4] {'tm'}, dimensions={0}, use_global_device_ids=true | all-gather | bytes 165888 | tf_op jit(solution)/shard_map/all_gather | solution.py:21
  100.2 30.6 %all-gather = f32[128,288]{1,0:T(8,128)S(1)} all-gather(f32[16,288]{1,0:T(8,128)S(1)} %get-tuple-element.1568), channel_id=2, replica_groups=mesh['tm'=8,'chan'=4] {'tm'}, dimensions={0}, use_global_device_ids=true | all-gather | bytes 165888 | tf_op jit(solution)/shard_map/all_gather | solution.py:21
  135.2 30.6 %all-gather.2 = f32[128,288]{1,0:T(8,128)S(1)} all-gather(f32[16,288]{1,0:T(8,128)S(1)} %get-tuple-element.593), channel_id=4, replica_groups=mesh['tm'=8,'chan'=4] {'tm'}, dimensions={0}, use_global_device_ids=true | all-gather | bytes 165888 | tf_op jit(solution)/shard_map/all_gather | solution.py:21
  166.6 16.4 %while.80 = (s32[]{:T(128)}, f32[16,288]{1,0:T(8,128)S(1)}, bf16[2,32,288]{2,1,0:T(8,128)(2,1)S(1)}, f32[2,32,288]{2,1,0:T(8,128)S(1)}, f32[2,32,288]{2,1,0:T(8,...) while((s32[]{:T(128)}, f32[16,288]{1,0:T(8,128)S(1)}, ...), condition=%wide.region_172.173_spmd, body=%wide.region_11.172_spmd.sunk | while | flops 3570210 | bytes 3898289 | solution.py:186
  183.1 10.2 %all-reduce.1 = (bf16[64,16]{0,1:T(8,128)(2,1)S(1)}, bf16[64,16]{0,1:T(8,128)(2,1)S(1)}) all-reduce(f32[64,16]{0,1:T(8,128)S(1)} %copy.182, f32[64,16]{0,1:T(8,128)S(1)} %copy.186), channel_id=1, replica_groups=mesh['tm'=8,'chan'=4] {'chan'}, use_global_device_ids=true, to_apply=%region_173.174 | all-reduce | flops 2048 | bytes 12288 | tf_op jit(solution)/shard_map/psum | solution.py:212
  198.2 5.7 %all-to-all-done.10 = bf16[32,2,16]{2,1,0:T(2,128)(2,1)S(1)} async-done(((bf16[32,2,16]{2,1,0:T(2,128)(2,1)}), bf16[32,2,16]{2,1,0:T(2,128)(2,1)S(1)}, u32[]{:S(2)}, u32[]{:S(2)}) %all-to-all-start.10) | async-done | bytes 2080 | tf_op jit(solution)/shard_map/all_to_all | solution.py:225
  209.2 4.5 %all-to-all-done.9 = bf16[32,2,16]{2,1,0:T(2,128)(2,1)S(1)} async-done(((bf16[32,2,16]{2,1,0:T(2,128)(2,1)}), bf16[32,2,16]{2,1,0:T(2,128)(2,1)S(1)}, u32[]{:S(2)}, u32[]{:S(2)}) %all-to-all-start.9) | async-done | bytes 2080 | tf_op jit(solution)/shard_map/all_to_all | solution.py:224
  213.7 3.3 %all-to-all-start.8 = ((bf16[32,2,288]{2,1,0:T(2,128)(2,1)}), bf16[32,2,288]{2,1,0:T(2,128)(2,1)S(1)}, u32[]{:S(2)}, u32[]{:S(2)}) async-start(bf16[32,2,288]{2,1,0:T(2,128)(2,1)} %copy.180), calls=%async_computation.8 | async-start | bytes 98304 | tf_op jit(solution)/shard_map/all_to_all | solution.py:223
  217.8 6.0 %all-to-all-done.8 = bf16[32,2,288]{2,1,0:T(2,128)(2,1)S(1)} async-done(((bf16[32,2,288]{2,1,0:T(2,128)(2,1)}), bf16[32,2,288]{2,1,0:T(2,128)(2,1)S(1)}, u32[]{:S(2)}, u32[]{:S(2)}) %all-to-all-start.8) | async-done | bytes 36896 | tf_op jit(solution)/shard_map/all_to_all | solution.py:223
  223.8 3.3 %all-to-all-start.7 = ((bf16[32,2,288]{2,1,0:T(2,128)(2,1)}), bf16[32,2,288]{2,1,0:T(2,128)(2,1)S(1)}, u32[]{:S(2)}, u32[]{:S(2)}) async-start(bf16[32,2,288]{2,1,0:T(2,128)(2,1)} %copy.178), calls=%async_computation.7 | async-start | bytes 98304 | tf_op jit(solution)/shard_map/all_to_all | solution.py:222
  227.9 6.0 %all-to-all-done.7 = bf16[32,2,288]{2,1,0:T(2,128)(2,1)S(1)} async-done(((bf16[32,2,288]{2,1,0:T(2,128)(2,1)}), bf16[32,2,288]{2,1,0:T(2,128)(2,1)S(1)}, u32[]{:S(2)}, u32[]{:S(2)}) %all-to-all-start.7) | async-done | bytes 36896 | tf_op jit(solution)/shard_map/all_to_all | solution.py:222
  233.9 3.3 %all-to-all-start.6 = ((bf16[32,2,288]{2,1,0:T(2,128)(2,1)}), bf16[32,2,288]{2,1,0:T(2,128)(2,1)S(1)}, u32[]{:S(2)}, u32[]{:S(2)}) async-start(bf16[32,2,288]{2,1,0:T(2,128)(2,1)} %copy.176), calls=%async_computation.6 | async-start | bytes 98304 | tf_op jit(solution)/shard_map/all_to_all | solution.py:221
  240.1 3.9 %all-to-all-done.6 = bf16[32,2,288]{2,1,0:T(2,128)(2,1)S(1)} async-done(((bf16[32,2,288]{2,1,0:T(2,128)(2,1)}), bf16[32,2,288]{2,1,0:T(2,128)(2,1)S(1)}, u32[]{:S(2)}, u32[]{:S(2)}) %all-to-all-start.6) | async-done | bytes 36896 | tf_op jit(solution)/shard_map/all_to_all | solution.py:221
  (378 shorter events, 55.8 us)
Async XLA Ops:
  2.1 7.4 %copy-start.7 = (bf16[64,16]{0,1:T(8,128)(2,1)S(1)}, bf16[64,16]{0,1:T(8,128)(2,1)}, u32[]{:S(2)}) copy-start(bf16[64,16]{0,1:T(8,128)(2,1)} %param.25) | copy-start | bytes 6148
  2.1 14.0 %all-to-all-start.5 = ((bf16[4,16,16]{2,0,1:T(4,128)(2,1)}), bf16[4,16,16]{2,0,1:T(4,128)(2,1)S(1)}, u32[]{:S(2)}, u32[]{:S(2)}) async-start(bf16[4,16,16]{2,0,1:T(4,128)(2,1)} %copy.173), calls=%async_computation.5 | async-start | bytes 32768 | tf_op jit(solution)/shard_map/all_to_all | solution.py:77
  9.6 9.9 %copy-start.1 = (bf16[64,288]{1,0:T(8,128)(2,1)S(1)}, bf16[64,288]{1,0:T(8,128)(2,1)}, u32[]{:S(2)}) copy-start(bf16[64,288]{1,0:T(8,128)(2,1)} %param.20) | copy-start | bytes 110596
  16.1 9.8 %all-to-all-start.1 = ((bf16[4,16,16]{2,0,1:T(4,128)(2,1)}), bf16[4,16,16]{2,0,1:T(4,128)(2,1)S(1)}, u32[]{:S(2)}, u32[]{:S(2)}) async-start(bf16[4,16,16]{2,0,1:T(4,128)(2,1)} %copy.162), calls=%async_computation.1 | async-start | bytes 32768 | tf_op jit(solution)/shard_map/all_to_all | solution.py:78
  19.4 0.8 copy-start.2
  20.2 0.8 copy-start.3
  21.0 0.8 copy-start.4
  25.9 10.1 %all-to-all-start.4 = ((bf16[4,16,288]{2,0,1:T(4,128)(2,1)}), bf16[4,16,288]{2,0,1:T(4,128)(2,1)S(1)}, u32[]{:S(2)}, u32[]{:S(2)}) async-start(bf16[4,16,288]{2,0,1:T(4,128)(2,1)} %copy.171), calls=%async_computation.4 | async-start | bytes 98304 | tf_op jit(solution)/shard_map/all_to_all | solution.py:73
  29.3 10.1 %copy-start.6 = (f32[4,288]{1,0:T(4,128)S(1)}, f32[4,288]{1,0:T(4,128)}, u32[]{:S(2)}) copy-start(f32[4,288]{1,0:T(4,128)} %param.26) | copy-start | bytes 13828
  36.0 10.1 %all-to-all-start.3 = ((bf16[4,16,288]{2,0,1:T(4,128)(2,1)}), bf16[4,16,288]{2,0,1:T(4,128)(2,1)S(1)}, u32[]{:S(2)}, u32[]{:S(2)}) async-start(bf16[4,16,288]{2,0,1:T(4,128)(2,1)} %copy.168), calls=%async_computation.3 | async-start | bytes 98304 | tf_op jit(solution)/shard_map/all_to_all | solution.py:75
  39.5 91.6 %collective-permute-start = (bf16[3,288]{1,0:T(4,128)(2,1)S(1)}, bf16[3,288]{1,0:T(4,128)(2,1)S(1)}, u32[]{:S(2)}, u32[]{:S(2)}) collective-permute-start(bf16[3,288]{1,0:T(4,128)(2,1)S(1)} %slice.3548), channel_id=1, source_target_pairs={{0,4},{4,8},{8,12},{12,16},{16,20},{20,24},{24,28},{1,5},{5,9},{9,... | collective-permute-start | bytes 5192 | tf_op jit(solution)/shard_map/ppermute | solution.py:14
  46.1 10.1 %all-to-all-start = ((bf16[4,16,288]{2,0,1:T(4,128)(2,1)}), bf16[4,16,288]{2,0,1:T(4,128)(2,1)S(1)}, u32[]{:S(2)}, u32[]{:S(2)}) async-start(bf16[4,16,288]{2,0,1:T(4,128)(2,1)} %copy.159), calls=%async_computation | async-start | bytes 98304 | tf_op jit(solution)/shard_map/all_to_all | solution.py:74
  56.2 10.1 %all-to-all-start.2 = ((bf16[4,16,288]{2,0,1:T(4,128)(2,1)}), bf16[4,16,288]{2,0,1:T(4,128)(2,1)S(1)}, u32[]{:S(2)}, u32[]{:S(2)}) async-start(bf16[4,16,288]{2,0,1:T(4,128)(2,1)} %copy.165), calls=%async_computation.2 | async-start | bytes 98304 | tf_op jit(solution)/shard_map/all_to_all | solution.py:76
  66.3 0.7 copy-start.5
  131.2 0.7 copy-start.8
  165.9 0.7 copy-start
  194.0 9.9 %all-to-all-start.10 = ((bf16[32,2,16]{2,1,0:T(2,128)(2,1)}), bf16[32,2,16]{2,1,0:T(2,128)(2,1)S(1)}, u32[]{:S(2)}, u32[]{:S(2)}) async-start(bf16[32,2,16]{2,1,0:T(2,128)(2,1)} %copy.187), calls=%async_computation.10 | async-start | bytes 32768 | tf_op jit(solution)/shard_map/all_to_all | solution.py:225
  203.9 9.9 %all-to-all-start.9 = ((bf16[32,2,16]{2,1,0:T(2,128)(2,1)}), bf16[32,2,16]{2,1,0:T(2,128)(2,1)S(1)}, u32[]{:S(2)}, u32[]{:S(2)}) async-start(bf16[32,2,16]{2,1,0:T(2,128)(2,1)} %copy.183), calls=%async_computation.9 | async-start | bytes 32768 | tf_op jit(solution)/shard_map/all_to_all | solution.py:224
  207.9 19.2 %collective-permute-start.1 = (f32[3,288]{1,0:T(4,128)S(1)}, f32[3,288]{1,0:T(4,128)S(1)}, u32[]{:S(2)}, u32[]{:S(2)}) collective-permute-start(f32[3,288]{1,0:T(4,128)S(1)} %slice.3554), channel_id=1, source_target_pairs={{4,0},{8,4},{12,8},{16,12},{20,16},{24,20},{28,24},{5,1},{9,5},{13... | collective-permute-start | bytes 10376 | tf_op jit(solution)/shard_map/ppermute | solution.py:14
  213.7 10.1 %all-to-all-start.8 = ((bf16[32,2,288]{2,1,0:T(2,128)(2,1)}), bf16[32,2,288]{2,1,0:T(2,128)(2,1)S(1)}, u32[]{:S(2)}, u32[]{:S(2)}) async-start(bf16[32,2,288]{2,1,0:T(2,128)(2,1)} %copy.180), calls=%async_computation.8 | async-start | bytes 98304 | tf_op jit(solution)/shard_map/all_to_all | solution.py:223
  223.8 10.1 %all-to-all-start.7 = ((bf16[32,2,288]{2,1,0:T(2,128)(2,1)}), bf16[32,2,288]{2,1,0:T(2,128)(2,1)S(1)}, u32[]{:S(2)}, u32[]{:S(2)}) async-start(bf16[32,2,288]{2,1,0:T(2,128)(2,1)} %copy.178), calls=%async_computation.7 | async-start | bytes 98304 | tf_op jit(solution)/shard_map/all_to_all | solution.py:222
  233.9 10.1 %all-to-all-start.6 = ((bf16[32,2,288]{2,1,0:T(2,128)(2,1)}), bf16[32,2,288]{2,1,0:T(2,128)(2,1)S(1)}, u32[]{:S(2)}, u32[]{:S(2)}) async-start(bf16[32,2,288]{2,1,0:T(2,128)(2,1)} %copy.176), calls=%async_computation.6 | async-start | bytes 98304 | tf_op jit(solution)/shard_map/all_to_all | solution.py:221
where the time goes:
time: 246 us; the launch traced here: 245 us
  blocking collectives  102 us (41%)
  waiting for transfers between devices  58.1 us (24%)
  starting transfers between devices  45.9 us (19%)
  local copies, waits for them, and re-layouts  21.4 us (9%)
  other arithmetic  14.5 us (6%)
    all_gather x3, blocking collectives, entering(): gathered = jax.tree.map(lambda a: lax.all_gather(a, axis), part)  91.9 us
    psum x1, blocking collectives, on_device(): sums_b, sums_c = lax.psum((part_b, part_c), 'chan')  10.2 us
    all_to_all x1, starting transfers between devices, on_device(): lax.all_to_all(to_frames(input_b), 'tm', split_axis=1, concat_axis=0, til...  7.38 us
    all_to_all x1, waiting for transfers between devices, on_device(): lax.all_to_all(to_frames(dt_raw), 'tm', split_axis=1, concat_axis=0, tile...  6.71 us
    all_to_all x1, waiting for transfers between devices, on_device(): lax.all_to_all(to_frames(inner_x), 'tm', split_axis=1, concat_axis=0, til...  6.71 us
    all_to_all x1, waiting for transfers between devices, on_device(): lax.all_to_all(to_frames(grad_out), 'tm', split_axis=1, concat_axis=0, ti...  6.59 us
    all_to_all x1, waiting for transfers between devices, on_device(): lax.all_to_all(from_seq(grad_sz), 'tm', split_axis=0, concat_axis=1, tile...  6.03 us
    all_to_all x1, waiting for transfers between devices, on_device(): lax.all_to_all(from_seq(grad_sdt), 'tm', split_axis=0, concat_axis=1, til...  6 us
  transfers between devices with their start and end apart: 13, of which 11 were waited for; matrix products, arithmetic and copies ran while one was open for 5% of the time, Pallas kernels for 0%

commit v1 on v0

v1 whole, which is shorter than its diff:
```python
import functools

import jax
import jax.numpy as jnp
from jax import lax
from jax.experimental import pallas as pl
from jax.experimental.pallas import tpu as pltpu
from jax.sharding import PartitionSpec as P

S_DEV = 2
BLK = 16
F32 = jnp.float32
BF16 = jnp.bfloat16
MESH = pl.DeviceIdType.MESH


def log2(value):
    assert value & (value - 1) == 0
    return value.bit_length() - 1


def dot(left, right):
    return jnp.dot(left, right, preferred_element_type=F32)


def iotas(shape):
    return lax.broadcasted_iota(jnp.int32, shape, 0), lax.broadcasted_iota(jnp.int32, shape, 1)


def ones_where(mask):
    return jnp.where(mask, 1.0, 0.0).astype(BF16)


def fields(packed, half, per, frames):
    partner = packed >> log2(2 * per)
    inside = packed & (2 * per - 1)
    rest = inside & (per - 1)
    spatial = rest >> log2(frames)
    frame = rest & (frames - 1)
    valid = (inside >> log2(per)) == half
    return partner, spatial, frame, valid


def row_of(packed, half, tm, per, frames):
    partner, spatial, frame, valid = fields(packed, half, per, frames)
    row = frame * (S_DEV * tm) + partner * S_DEV + spatial
    return jnp.where(valid, row, -1)


def place_of(packed, half, tm, per, frames):
    partner, spatial, frame, valid = fields(packed, half, per, frames)
    place = spatial * (frames * tm) + partner * frames + frame
    return jnp.where(valid, place, -1)


def pack_matrix(of, half, tm, per, frames, length):
    packed, row = iotas((tm * 2 * per, length))
    return ones_where(of(packed, half, tm, per, frames) == row)


def unpack_matrix(of, half, tm, per, frames, length):
    row, packed = iotas((length, tm * 2 * per))
    return ones_where(of(packed, half, tm, per, frames) == row)


def sigmoid(values):
    return 1.0 / (1.0 + jnp.exp(-values))


def silu_grad(values):
    sigm = sigmoid(values)
    return sigm * (1.0 + values * (1.0 - sigm))


def kernel(
    tm,
    chan,
    x_ref,
    z_ref,
    dt_ref,
    g_ref,
    b_ref,
    c_ref,
    w_ref,
    bias_ref,
    log_ref,
    skip_ref,
    out_a,
    out_b,
    send_1,
    send_2,
    send_h,
    recv_1,
    recv_2,
    recv_h,
    ends,
    ends_in,
    part,
    part_in,
    edge,
    edge_in,
    send_a,
    send_b,
    xpad,
    pre_s,
    conv_s,
    delta_s,
    u_s,
    dy_s,
    dt_s,
    z_s,
    g_s,
    y_s,
    w_s,
    d_s,
    gp_s,
    bc_s,
    fs_s,
    prod,
    sem_1,
    sem_2,
    sem_h,
    sem_e,
    sem_p,
    sem_g,
    sem_a,
    sem_b,
):
    me = lax.axis_index("tm")
    ch = lax.axis_index("chan")
    length, width = x_ref.shape
    states = b_ref.shape[1]
    taps = w_ref.shape[0]
    frames = length // (S_DEV * tm)
    per = S_DEV * frames
    wide = width + 2 * states
    base = width // 128 * 128

    def partner(k):
        return lax.rem(me + k, tm)

    def peer(k):
        return lax.rem(ch + k, chan)

    def over_tm(body):
        def step(k, carry):
            body(partner(k))
            return carry

        lax.fori_loop(1, tm, step, 0)

    def over_chan(body):
        for k in range(1, chan):
            body(peer(k))

    barrier = pltpu.get_barrier_semaphore()

    def greet(d):
        pl.semaphore_signal(barrier, inc=1, device_id={"tm": d}, device_id_type=MESH)

    def greet_peer(d):
        pl.semaphore_signal(barrier, inc=1, device_id={"chan": d}, device_id_type=MESH)

    over_tm(greet)
    over_chan(greet_peer)

    row, lane = iotas((width, wide))
    ex = ones_where(row == lane)
    row, lane = iotas((states, wide))
    eb = ones_where(lane == row + width)
    ec = ones_where(lane == row + width + states)
    x_ext = (dot(x_ref[...], ex) + dot(b_ref[...], eb) + dot(c_ref[...], ec)).astype(BF16)
    first = pack_matrix(row_of, 0, tm, per, frames, length)
    second = pack_matrix(row_of, 1, tm, per, frames, length)
    dt_ext = dot(dt_ref[...], ex).astype(BF16)
    one = (dot(first, x_ext) + dot(second, dt_ext)).astype(BF16)
    two = (dot(first, z_ref[...]) + dot(second, g_ref[...])).astype(BF16)
    send_1[...] = one.reshape(tm, 2 * per, wide)
    send_2[...] = two.reshape(tm, 2 * per, width)
    packed, row = iotas((tm * 16, length))
    slot = packed & 15
    frame = slot - (8 - frames)
    source = frame * (S_DEV * tm) + (packed >> 4) * S_DEV - 1
    good = (frame >= 0) & (slot < 8) & (packed >= 16)
    halo = ones_where(jnp.where(good, source, -1) == row)
    send_h[...] = dot(halo, x_ref[...]).astype(BF16).reshape(tm, 16, width)

    pl.semaphore_wait(barrier, tm - 1 + chan - 1)

    def copy_tm(src, dst, sems, d, origin):
        return pltpu.make_async_remote_copy(
            src_ref=src,
            dst_ref=dst,
            send_sem=sems.at[0, d],
            recv_sem=sems.at[1, origin],
            device_id={"tm": d},
            device_id_type=MESH,
        )

    def copy_1(d, origin):
        return copy_tm(send_1.at[d], recv_1.at[origin], sem_1, d, origin)

    def copy_2(d, origin):
        return copy_tm(send_2.at[d], recv_2.at[origin], sem_2, d, origin)

    def copy_h(d):
        return pltpu.make_async_remote_copy(
            src_ref=send_h.at[d],
            dst_ref=recv_h,
            send_sem=sem_h.at[d],
            recv_sem=sem_h.at[tm],
            device_id={"tm": d},
            device_id_type=MESH,
        )

    def start_halo(d):
        @pl.when(me == tm - 1)
        def _():
            copy_h(d).start()

    over_tm(start_halo)
    over_tm(lambda d: copy_1(d, me).start())
    over_tm(lambda d: copy_2(d, me).start())
    recv_1[me] = send_1[me]
    recv_2[me] = send_2[me]

    rate = -jnp.exp(log_ref[...])
    take_0 = unpack_matrix(place_of, 0, tm, per, frames, length)
    take_1 = unpack_matrix(place_of, 1, tm, per, frames, length)
    row, lane = iotas((BLK, BLK * states))
    sel = ones_where((lane >> log2(states)) == row)
    row, lane = iotas((BLK * states, BLK))
    spread = ones_where((row >> log2(states)) == lane)

    @pl.when(me == tm - 1)
    def _():
        recv_h[...] = send_h[me]

    @pl.when(me != tm - 1)
    def _():
        copy_h(me).wait_recv()

    over_tm(lambda d: copy_1(d, d).wait_recv())
    got_1 = recv_1[...].reshape(tm * 2 * per, wide)
    x_full = dot(take_0, got_1)
    dt_vals = dot(take_1, got_1[:, :width])
    xpad[0:8, :] = recv_h[...].astype(F32)[0:8]
    xpad[8:, :] = x_full[:, :width]
    tail = wide - base
    bc_bf = x_full[:, base:].astype(BF16)
    row, lane = iotas((BLK * states, tail))
    keep = ((lane - (width - base)) & (states - 1)) == (row & (states - 1))
    keep = keep & (lane >= width - base)
    row, lane = iotas((tail, 256))
    fan = ones_where(
        (row >= width - base)
        & (((row - (width - base)) >> log2(states)) == (lane >> 7))
    )
    for block in range(length // BLK):
        rows = dot(spread, bc_bf[block * BLK : (block + 1) * BLK])
        rows = jnp.where(keep, rows, 0.0).astype(BF16)
        bc_s[block * BLK * states : (block + 1) * BLK * states, :] = dot(rows, fan)

    dt_s[...] = dt_vals
    deltas = jnp.maximum(dt_vals, 0.0) + jnp.log(1.0 + jnp.exp(-jnp.abs(dt_vals)))
    delta_s[...] = deltas
    pre = bias_ref[...] + w_ref[0:1, :] * xpad[8 - taps + 1 : 8 - taps + 1 + length, :]
    for k in range(1, taps):
        pre = pre + w_ref[k : k + 1, :] * xpad[8 - taps + 1 + k : 8 - taps + 1 + k + length, :]
    pre_s[...] = pre
    conv = pre * sigmoid(pre)
    conv_s[...] = conv
    u_s[...] = deltas * conv
    total = jnp.sum(deltas, axis=0, keepdims=True)

    over_tm(lambda d: copy_2(d, d).wait_recv())
    got_2 = recv_2[...].reshape(tm * 2 * per, width)
    z_vals = dot(take_0, got_2)
    g_vals = dot(take_1, got_2)
    z_s[...] = z_vals
    g_s[...] = g_vals
    dy_s[...] = (g_vals * (z_vals * sigmoid(z_vals))).astype(BF16).astype(F32)

    def over_lanes(tile):
        return jnp.concatenate([tile] * (width // 128) + [tile[:, : width % 128]], axis=1)

    def b_at(q):
        return over_lanes(bc_s[pl.ds(pl.multiple_of(q * states, states), states), 0:128])

    def c_at(q):
        return over_lanes(bc_s[pl.ds(pl.multiple_of(q * states, states), states), 128:256])

    zero = jnp.zeros((states, width), F32)

    def local(i, carry):
        state, back = carry
        up = pl.multiple_of(i * 8, 8)
        down = pl.multiple_of(length - 8 - i * 8, 8)
        d_up, u_up = delta_s[pl.ds(up, 8), :], u_s[pl.ds(up, 8), :]
        d_dn, y_dn = delta_s[pl.ds(down, 8), :], dy_s[pl.ds(down, 8), :]
        for j in range(8):
            state = jnp.exp(d_up[j : j + 1] * rate) * state + u_up[j : j + 1] * b_at(up + j)
            m = 7 - j
            back = jnp.exp(d_dn[m : m + 1] * rate) * (y_dn[m : m + 1] * c_at(down + m) + back)
        return state, back

    end, back_end = lax.fori_loop(0, length // 8, local, (zero, zero))
    row = lax.broadcasted_iota(jnp.int32, (16, width), 0)
    high = total.astype(BF16).astype(F32)
    sums = jnp.where(row == 0, high, jnp.where(row == 1, total - high, 0.0))
    ends[0:16, :] = end.astype(BF16)
    ends[16:32, :] = sums.astype(BF16)
    ends[32:48, :] = back_end.astype(BF16)

    def copy_up(d, origin):
        return copy_tm(ends.at[0:32], ends_in.at[origin, 0:32], sem_e, d, origin)

    def copy_down(d, origin):
        return copy_tm(ends.at[16:48], ends_in.at[origin, 16:48], sem_e, d, origin)

    def send_end(d):
        @pl.when(d > me)
        def _():
            copy_up(d, me).start()

        @pl.when(d < me)
        def _():
            copy_down(d, me).start()

    over_tm(send_end)

    def through(source):
        pair = ends_in[source, 16:32, :].astype(F32)
        return jnp.exp(rate * (pair[0:1] + pair[1:2]))

    def enter_up(source, state):
        copy_up(source, source).wait_recv()
        return through(source) * state + ends_in[source, 0:16, :].astype(F32)

    def enter_down(turn, back):
        source = tm - 1 - turn
        copy_down(source, source).wait_recv()
        return through(source) * back + ends_in[source, 32:48, :].astype(F32)

    state_in = lax.fori_loop(0, me, enter_up, zero)
    back_in = lax.fori_loop(0, tm - 1 - me, enter_down, zero)

    row, lane = iotas((BLK * states, 128))
    at_b = lane == (row & (states - 1))
    at_c = lane == (row & (states - 1)) + states
    ones = jnp.ones((width, 128), BF16)
    skip = skip_ref[...]

    def picked(product, where):
        sums = jnp.where(where, dot(product, ones), 0.0)
        high = sums.astype(BF16)
        low = (sums - high.astype(F32)).astype(BF16)
        return dot(sel, high) + dot(sel, low)

    def forward(i, state):
        start = pl.multiple_of(i * BLK, BLK)
        here = pl.ds(start, BLK)
        d_blk, u_blk, y_blk = delta_s[here, :], u_s[here, :], dy_s[here, :]
        for j in range(BLK):
            kept = jnp.exp(d_blk[j : j + 1] * rate) * state
            state = kept + u_blk[j : j + 1] * b_at(start + j)
            fs_s[pl.ds(pl.multiple_of((start + j) * states, states), states), :] = kept
            prod[0, j * states : (j + 1) * states, :] = (c_at(start + j) * state).astype(BF16)
            prod[1, j * states : (j + 1) * states, :] = (y_blk[j : j + 1] * state).astype(BF16)
        y_s[here, :] = dot(sel, prod[0]) + skip * conv_s[here, :]
        part[here, :] = picked(prod[1], at_c)
        return state

    lax.fori_loop(0, length // BLK, forward, state_in)

    def backward(turn, back):
        start = pl.multiple_of(length - BLK - turn * BLK, BLK)
        here = pl.ds(start, BLK)
        d_blk, u_blk, y_blk = delta_s[here, :], u_s[here, :], dy_s[here, :]
        for j in reversed(range(BLK)):
            adjoint = y_blk[j : j + 1] * c_at(start + j) + back
            back = jnp.exp(d_blk[j : j + 1] * rate) * adjoint
            kept = fs_s[pl.ds(pl.multiple_of((start + j) * states, states), states), :]
            rows = slice(j * states, (j + 1) * states)
            prod[0, rows, :] = (adjoint * b_at(start + j)).astype(BF16)
            prod[1, rows, :] = (adjoint * u_blk[j : j + 1]).astype(BF16)
            prod[2, rows, :] = (adjoint * rate * kept).astype(BF16)
        w_s[here, :] = dot(sel, prod[0])
        d_s[here, :] = dot(sel, prod[2])
        part[here, :] = part[here, :] + picked(prod[1], at_b)
        return back

    lax.fori_loop(0, length // BLK, backward, back_in)

    def copy_part(d, origin):
        return pltpu.make_async_remote_copy(
            src_ref=part,
            dst_ref=part_in.at[origin],
            send_sem=sem_p.at[0, d],
            recv_sem=sem_p.at[1, origin],
            device_id={"chan": d},
            device_id_type=MESH,
        )

    over_chan(lambda d: copy_part(d, ch).start())
    deltas = delta_s[...]
    weighted = w_s[...]
    grad_pre = (skip * dy_s[...] + deltas * weighted) * silu_grad(pre_s[...])
    gp_s[0:length, :] = grad_pre
    edge[...] = grad_pre[0:8]

    def copy_edge(d):
        return pltpu.make_async_remote_copy(
            src_ref=edge,
            dst_ref=edge_in,
            send_sem=sem_g.at[0],
            recv_sem=sem_g.at[1],
            device_id={"tm": d},
            device_id_type=MESH,
        )

    before = jnp.maximum(me - 1, 0)

    @pl.when(me > 0)
    def _():
        copy_edge(before).start()

    give_0 = pack_matrix(place_of, 0, tm, per, frames, length)
    give_1 = pack_matrix(place_of, 1, tm, per, frames, length)
    grad_dt = ((d_s[...] + conv_s[...] * weighted) * sigmoid(dt_s[...])).astype(BF16)
    seq_y = y_s[...].astype(BF16).astype(F32)
    grad_z = (g_s[...] * seq_y * silu_grad(z_s[...])).astype(BF16)
    both = (dot(give_0, grad_dt) + dot(give_1, grad_z)).astype(BF16)
    send_a[...] = both.reshape(tm, 2 * per, width)

    def copy_a(d, origin):
        return copy_tm(send_a.at[d], out_a.at[origin], sem_a, d, origin)

    def copy_b(d, origin):
        return copy_tm(send_b.at[d], out_b.at[origin], sem_b, d, origin)

    over_tm(lambda d: copy_a(d, me).start())
    out_a[me] = send_a[me]

    @pl.when(me < tm - 1)
    def _():
        copy_edge(before).wait_recv()
        gp_s[length:, :] = edge_in[...]

    @pl.when(me == tm - 1)
    def _():
        gp_s[length:, :] = jnp.zeros((8, width), F32)

    grad_x = w_ref[0:1, :] * gp_s[taps - 1 : taps - 1 + length, :]
    for k in range(1, taps):
        grad_x = grad_x + w_ref[k : k + 1, :] * gp_s[taps - 1 - k : taps - 1 - k + length, :]
    x_part = dot(give_0, grad_x.astype(BF16))
    over_chan(lambda d: copy_part(d, d).wait_recv())
    part_in[ch] = part[...]
    bc = part_in[0]
    for k in range(1, chan):
        bc = bc + part_in[k]
    bc = jnp.concatenate([bc.astype(BF16), jnp.zeros((length, width - 128), BF16)], axis=1)
    send_b[...] = (x_part + dot(give_1, bc)).astype(BF16).reshape(tm, 2 * per, width)
    over_tm(lambda d: copy_b(d, me).start())
    out_b[me] = send_b[me]

    over_tm(lambda d: copy_1(d, me).wait_send())
    over_tm(lambda d: copy_2(d, me).wait_send())

    def end_halo(d):
        @pl.when(me == tm - 1)
        def _():
            copy_h(d).wait_send()

    over_tm(end_halo)

    def end_ends(d):
        @pl.when(d > me)
        def _():
            copy_up(d, me).wait_send()

        @pl.when(d < me)
        def _():
            copy_down(d, me).wait_send()

    over_tm(end_ends)
    over_chan(lambda d: copy_part(d, ch).wait_send())

    @pl.when(me > 0)
    def _():
        copy_edge(before).wait_send()

    over_tm(lambda d: copy_a(d, me).wait_send())
    over_tm(lambda d: copy_b(d, me).wait_send())
    over_tm(lambda d: copy_a(d, d).wait_recv())
    over_tm(lambda d: copy_b(d, d).wait_recv())


def unpack_kernel(tm, states, a_ref, b_ref, gx_ref, gdt_ref, gz_ref, gb_ref, gc_ref):
    length, width = gx_ref.shape
    frames = length // (S_DEV * tm)
    per = S_DEV * frames
    take_0 = unpack_matrix(row_of, 0, tm, per, frames, length)
    take_1 = unpack_matrix(row_of, 1, tm, per, frames, length)
    got_a = a_ref[...].reshape(tm * 2 * per, width)
    got_b = b_ref[...].reshape(tm * 2 * per, width)
    gdt_ref[...] = dot(take_0, got_a).astype(BF16)
    gz_ref[...] = dot(take_1, got_a).astype(BF16)
    gx_ref[...] = dot(take_0, got_b).astype(BF16)
    bc = dot(take_1, got_b[:, 0:128]).astype(BF16)
    row, lane = iotas((128, states))
    gb_ref[...] = dot(bc, ones_where(row == lane)).astype(BF16)
    gc_ref[...] = dot(bc, ones_where(row == lane + states)).astype(BF16)


def on_device(
    tm,
    chan,
    inner_x,
    gate_z,
    dt_raw,
    grad_out,
    input_b,
    output_c,
    conv_weight,
    conv_bias,
    decay_log,
    skip_gain,
):
    length, width = inner_x.shape
    states = input_b.shape[1]
    per = length // tm
    wide = width + 2 * states
    vmem = pl.BlockSpec(memory_space=pltpu.VMEM)
    rows = pltpu.VMEM((length, width), F32)
    block = (tm, 2 * per, width)
    sems = pltpu.SemaphoreType.DMA
    limit = 60 * 1024 * 1024
    scratch = [
        pltpu.VMEM((tm, 2 * per, wide), BF16),
        pltpu.VMEM(block, BF16),
        pltpu.VMEM((tm, 16, width), BF16),
        pltpu.VMEM((tm, 2 * per, wide), BF16),
        pltpu.VMEM(block, BF16),
        pltpu.VMEM((16, width), BF16),
        pltpu.VMEM((48, width), BF16),
        pltpu.VMEM((tm, 48, width), BF16),
        pltpu.VMEM((length, 128), F32),
        pltpu.VMEM((chan, length, 128), F32),
        pltpu.VMEM((8, width), F32),
        pltpu.VMEM((8, width), F32),
        pltpu.VMEM(block, BF16),
        pltpu.VMEM(block, BF16),
        pltpu.VMEM((length + 8, width), F32),
        *[rows] * 11,
        pltpu.VMEM((length + 8, width), F32),
        pltpu.VMEM((length * states, 256), F32),
        pltpu.VMEM((length * states, width), F32),
        pltpu.VMEM((3, BLK * states, width), BF16),
        sems((2, tm)),
        sems((2, tm)),
        sems((tm + 1,)),
        sems((2, tm)),
        sems((2, chan)),
        sems((2,)),
        sems((2, tm)),
        sems((2, tm)),
    ]
    out_a, out_b = pl.pallas_call(
        functools.partial(kernel, tm, chan),
        out_shape=[jax.ShapeDtypeStruct(block, BF16)] * 2,
        in_specs=[vmem] * 10,
        out_specs=[vmem] * 2,
        scratch_shapes=scratch,
        compiler_params=pltpu.CompilerParams(
            collective_id=0, has_side_effects=True, vmem_limit_bytes=limit
        ),
    )(
        inner_x,
        gate_z,
        dt_raw,
        grad_out,
        input_b,
        output_c,
        conv_weight,
        conv_bias.reshape(1, width),
        decay_log,
        skip_gain.reshape(1, width),
    )
    wide_out = jax.ShapeDtypeStruct((length, width), BF16)
    thin_out = jax.ShapeDtypeStruct((length, states), BF16)
    return pl.pallas_call(
        functools.partial(unpack_kernel, tm, states),
        out_shape=[wide_out, wide_out, wide_out, thin_out, thin_out],
        in_specs=[vmem] * 2,
        out_specs=[vmem] * 5,
        compiler_params=pltpu.CompilerParams(vmem_limit_bytes=limit),
    )(out_a, out_b)


def solution(mesh):
    return jax.shard_map(
        functools.partial(on_device, mesh.shape["tm"], mesh.shape["chan"]),
        mesh=mesh,
        in_specs=(
            P("tm", "chan"),
            P("tm", "chan"),
            P("tm", "chan"),
            P("tm", "chan"),
            P("tm", None),
            P("tm", None),
            P(None, "chan"),
            P("chan"),
            P(None, "chan"),
            P("chan"),
        ),
        out_specs=(P("tm", "chan"), P("tm", "chan"), P("tm", "chan"), P("tm", None), P("tm", None)),
        check_vma=False,
    )
```

time: 246 us -> 41.3 us (0.17)
  blocking collectives: 102 us -> 0 us
  waiting for transfers between devices: 58.1 us -> 0 us
  starting transfers between devices: 45.9 us -> 0 us
  Pallas kernels: 0 us -> 35 us
  local copies, waits for them, and re-layouts: 21.4 us -> 5.29 us
  other arithmetic: 14.5 us -> 0 us
    all_gather x3 -> x0, blocking collectives: 91.9 us -> none  [entering(): gathered = jax.tree.map(lambda a: lax.all_gather(a, axis), part)]
    all_to_all x11 -> x0, waiting for transfers between devices: 58.1 us -> none  [the longest x1 6.71 us: on_device(): lax.all_to_all(to_frames(dt_raw), 'tm', split_axis=1, concat_axis=0, tile...]
    all_to_all x11 -> x0, starting transfers between devices: 40.8 us -> none  [the longest x1 7.38 us: on_device(): lax.all_to_all(to_frames(input_b), 'tm', split_axis=1, concat_axis=0, til...]
    pallas_call x0 -> x2, Pallas kernels: none -> 35 us  [the longest x1 33.2 us: on_device(): pl.pallas_call(functools.partial(kernel, tm, chan), out_shape=[jax.ShapeD...]
    reduce_sum x51 -> x0, other arithmetic: 10.2 us -> none  [the longest x14 3.54 us: backward_block(): jnp.sum(adjoint * decay_rate * decays[offset] * previous[offset], axis=0)]
    psum x1 -> x0, blocking collectives: 10.2 us -> none  [on_device(): sums_b, sums_c = lax.psum((part_b, part_c), 'chan')]
    reshape x15 -> x2, local copies, waits for them, and re-layouts: 7.08 us -> 1.82 us  [the longest x1 1.26 us: on_device(): conv_bias.reshape(1, width)]
    ppermute x2 -> x0, starting transfers between devices: 5.09 us -> none  [from_behind(): lax.ppermute(value, axis, [(source, source + steps) for source in range(i...]
  transfers between devices with their start and end apart: 13 -> 0, of which waited for: 11 -> 0; matrix products, arithmetic and copies ran while one was open for 5% -> 0% of each run, Pallas kernels for 0% -> 0%
where the time goes in v1:
time: 41.3 us; the launch traced here: 41 us
  Pallas kernels  35 us (85%)
  local copies, waits for them, and re-layouts  5.29 us (13%)
  between operations  0.66 us (2%)
    pallas_call x1, Pallas kernels, on_device(): pl.pallas_call(functools.partial(kernel, tm, chan), out_shape=[jax.ShapeD...  33.2 us
    pallas_call x2, local copies, waits for them, and re-layouts, on_device(): pl.pallas_call(functools.partial(unpack_kernel, tm, states), out_shape=[w...  2.06 us
    pallas_call x1, Pallas kernels, on_device(): pl.pallas_call(functools.partial(unpack_kernel, tm, states), out_shape=[w...  1.88 us
    unnamed x10, local copies, waits for them, and re-layouts  1.41 us
    reshape x1, local copies, waits for them, and re-layouts, on_device(): conv_bias.reshape(1, width)  1.26 us

profile of v1, /device:TPU:0, one launch (start us, length us, event | category | flops | bytes accessed | tf_op | source)
XLA Modules:
  0.0 41.0 jit_solution(17072352921208008830)
XLA Ops:
  0.6 0.0 copy-start.3
  0.6 0.0 copy-start.1
  0.7 1.3 %reshape.16.bias_ref = f32[1,288]{1,0:T(1,128)} reshape(f32[288]{0:T(512)} %param.17) | data formatting | bytes 2304 | tf_op jit(solution)/shard_map/reshape | solution.py:587
  1.9 0.0 copy-done.3
  1.9 0.6 %reshape.17.skip_ref = f32[1,288]{1,0:T(1,128)} reshape(f32[288]{0:T(512)S(1)} %copy-done.3) | data formatting | bytes 2304 | tf_op jit(solution)/shard_map/reshape | solution.py:589
  2.5 0.0 copy-done.1
  2.5 0.0 copy-start.2
  2.5 0.7 %copy.15.b_ref = bf16[64,16]{1,0:T(8,128)(2,1)} copy(bf16[64,16]{0,1:T(8,128)(2,1)S(1)} %copy-done.1) | data formatting | bytes 4096 | tf_op args[4]
  3.2 0.0 copy-done.2
  3.2 0.7 %copy.16.c_ref = bf16[64,16]{1,0:T(8,128)(2,1)} copy(bf16[64,16]{0,1:T(8,128)(2,1)S(1)} %copy-done.2) | data formatting | bytes 4096 | tf_op args[5]
  3.9 33.2 %shard_map.137 = (bf16[8,16,288]{2,1,0:T(8,128)(2,1)}, bf16[8,16,288]{2,1,0:T(8,128)(2,1)}) custom-call(bf16[64,288]{1,0:T(8,128)(2,1)} %x_ref.1, bf16[64,288]{1,0:T(8,128)(2,1)} %z_ref.1, bf16[64,288]{1,0:T(8,128)(2,1)} %dt_ref.1, bf16[64,288]{1,0:T(8,128)(2,1)} %g_ref.1, bf16[64,16]{1,0:T(8,128)(2,1)} %copy.15.b_ref, bf16[64,16]{1,0:T(8,128)(2,1)} %copy.16.c_ref, ...), custom_call_target="tpu_custom_call" | custom-call | tf_op jit(solution)/shard_map/pallas_call | solution.py:570
  37.0 1.9 %shard_map.138 = (bf16[64,288]{1,0:T(8,128)(2,1)}, bf16[64,288]{1,0:T(8,128)(2,1)}, bf16[64,288]{1,0:T(8,128)(2,1)}, bf16[64,16]{1,0:T(8,128)(2,1)}, bf16[64,16]{1,0:T(8,128)(2,1)}) custom-call(bf16[8,16,288]{2,1,0:T(8,128)(2,1)} %get-tuple-element.7.a_ref, bf16[8,16,288]{2,1,0:T(8,128)(2,1)} %get-tuple-element.8.b_ref), custom_call_target="tpu_custom_call" | custom-call | tf_op jit(solution)/shard_map/pallas_call | solution.py:593
  38.9 0.0 copy-start
  38.9 1.4 %copy.17 = bf16[64,16]{0,1:T(8,128)(2,1)} copy(bf16[64,16]{1,0:T(8,128)(2,1)} %get-tuple-element.12) | data formatting | bytes 4096 | tf_op jit(solution)/shard_map/pallas_call | solution.py:593
  40.3 0.0 copy-done
  40.3 0.7 %copy.18 = bf16[64,16]{0,1:T(8,128)(2,1)} copy(bf16[64,16]{1,0:T(8,128)(2,1)S(1)} %copy-done) | data formatting | bytes 4096 | tf_op jit(solution)/shard_map/pallas_call | solution.py:593
Async XLA Ops:
  0.6 1.3 %copy-start.3 = (f32[288]{0:T(512)S(1)}, f32[288]{0:T(512)}, u32[]{:S(2)}) copy-start(f32[288]{0:T(512)} %param.19) | copy-start | bytes 3460
  0.6 1.8 %copy-start.1 = (bf16[64,16]{0,1:T(8,128)(2,1)S(1)}, bf16[64,16]{0,1:T(8,128)(2,1)}, u32[]{:S(2)}) copy-start(bf16[64,16]{0,1:T(8,128)(2,1)} %param.14) | copy-start | bytes 6148
  2.5 0.7 %copy-start.2 = (bf16[64,16]{0,1:T(8,128)(2,1)S(1)}, bf16[64,16]{0,1:T(8,128)(2,1)}, u32[]{:S(2)}) copy-start(bf16[64,16]{0,1:T(8,128)(2,1)} %param.15) | copy-start | bytes 6148
  38.9 1.4 %copy-start = (bf16[64,16]{1,0:T(8,128)(2,1)S(1)}, bf16[64,16]{1,0:T(8,128)(2,1)}, u32[]{:S(2)}) copy-start(bf16[64,16]{1,0:T(8,128)(2,1)} %get-tuple-element.13) | copy-start | bytes 6148

commit v2 on v1

--- a/solution.py
+++ b/solution.py
@@ -21,6 +21,10 @@
 
 def dot(left, right):
     return jnp.dot(left, right, preferred_element_type=F32)
+
+
+def dot_t(left, right):
+    return lax.dot_general(left, right, (((1,), (1,)), ((), ())), preferred_element_type=F32)
 
 
 def iotas(shape):
@@ -129,7 +133,7 @@
     me = lax.axis_index("tm")
     ch = lax.axis_index("chan")
     length, width = x_ref.shape
-    states = b_ref.shape[1]
+    states = b_ref.shape[0]
     taps = w_ref.shape[0]
     frames = length // (S_DEV * tm)
     per = S_DEV * frames
@@ -169,14 +173,14 @@
     row, lane = iotas((states, wide))
     eb = ones_where(lane == row + width)
     ec = ones_where(lane == row + width + states)
-    x_ext = (dot(x_ref[...], ex) + dot(b_ref[...], eb) + dot(c_ref[...], ec)).astype(BF16)
+    x_ext = dot(x_ref[...], ex).astype(BF16)
     first = pack_matrix(row_of, 0, tm, per, frames, length)
     second = pack_matrix(row_of, 1, tm, per, frames, length)
     dt_ext = dot(dt_ref[...], ex).astype(BF16)
-    one = (dot(first, x_ext) + dot(second, dt_ext)).astype(BF16)
-    two = (dot(first, z_ref[...]) + dot(second, g_ref[...])).astype(BF16)
-    send_1[...] = one.reshape(tm, 2 * per, wide)
-    send_2[...] = two.reshape(tm, 2 * per, width)
+    b_rows = dot_t(first, b_ref[...]).astype(BF16)
+    c_rows = dot_t(first, c_ref[...]).astype(BF16)
+    one = dot(first, x_ext) + dot(second, dt_ext) + dot(b_rows, eb) + dot(c_rows, ec)
+    send_1[...] = one.astype(BF16).reshape(tm, 2 * per, wide)
     packed, row = iotas((tm * 16, length))
     slot = packed & 15
     frame = slot - (8 - frames)
@@ -184,8 +188,6 @@
     good = (frame >= 0) & (slot < 8) & (packed >= 16)
     halo = ones_where(jnp.where(good, source, -1) == row)
     send_h[...] = dot(halo, x_ref[...]).astype(BF16).reshape(tm, 16, width)
-
-    pl.semaphore_wait(barrier, tm - 1 + chan - 1)
 
     def copy_tm(src, dst, sems, d, origin):
         return pltpu.make_async_remote_copy(
@@ -218,8 +220,11 @@
         def _():
             copy_h(d).start()
 
+    pl.semaphore_wait(barrier, tm - 1 + chan - 1)
     over_tm(start_halo)
     over_tm(lambda d: copy_1(d, me).start())
+    two = dot(first, z_ref[...]) + dot(second, g_ref[...])
+    send_2[...] = two.astype(BF16).reshape(tm, 2 * per, width)
     over_tm(lambda d: copy_2(d, me).start())
     recv_1[me] = send_1[me]
     recv_2[me] = send_2[me]
@@ -264,7 +269,7 @@
     dt_s[...] = dt_vals
     deltas = jnp.maximum(dt_vals, 0.0) + jnp.log(1.0 + jnp.exp(-jnp.abs(dt_vals)))
     delta_s[...] = deltas
-    pre = bias_ref[...] + w_ref[0:1, :] * xpad[8 - taps + 1 : 8 - taps + 1 + length, :]
+    pre = bias_ref[...].reshape(1, width) + w_ref[0:1, :] * xpad[8 - taps + 1 : 8 - taps + 1 + length, :]
     for k in range(1, taps):
         pre = pre + w_ref[k : k + 1, :] * xpad[8 - taps + 1 + k : 8 - taps + 1 + k + length, :]
     pre_s[...] = pre
@@ -349,7 +354,7 @@
     at_b = lane == (row & (states - 1))
     at_c = lane == (row & (states - 1)) + states
     ones = jnp.ones((width, 128), BF16)
-    skip = skip_ref[...]
+    skip = skip_ref[...].reshape(1, width)
 
     def picked(product, where):
         sums = jnp.where(where, dot(product, ones), 0.0)
@@ -509,9 +514,9 @@
     gz_ref[...] = dot(take_1, got_a).astype(BF16)
     gx_ref[...] = dot(take_0, got_b).astype(BF16)
     bc = dot(take_1, got_b[:, 0:128]).astype(BF16)
-    row, lane = iotas((128, states))
-    gb_ref[...] = dot(bc, ones_where(row == lane)).astype(BF16)
-    gc_ref[...] = dot(bc, ones_where(row == lane + states)).astype(BF16)
+    row, lane = iotas((states, 128))
+    gb_ref[...] = dot_t(ones_where(row == lane), bc).astype(BF16)
+    gc_ref[...] = dot_t(ones_where(row + states == lane), bc).astype(BF16)
 
 
 def on_device(
@@ -581,22 +586,23 @@
         gate_z,
         dt_raw,
         grad_out,
-        input_b,
-        output_c,
+        input_b.T,
+        output_c.T,
         conv_weight,
-        conv_bias.reshape(1, width),
+        conv_bias,
         decay_log,
-        skip_gain.reshape(1, width),
+        skip_gain,
     )
     wide_out = jax.ShapeDtypeStruct((length, width), BF16)
-    thin_out = jax.ShapeDtypeStruct((length, states), BF16)
-    return pl.pallas_call(
+    thin_out = jax.ShapeDtypeStruct((states, length), BF16)
+    gx, gdt, gz, gb, gc = pl.pallas_call(
         functools.partial(unpack_kernel, tm, states),
         out_shape=[wide_out, wide_out, wide_out, thin_out, thin_out],
         in_specs=[vmem] * 2,
         out_specs=[vmem] * 5,
         compiler_params=pltpu.CompilerParams(vmem_limit_bytes=limit),
     )(out_a, out_b)
+    return gx, gdt, gz, gb.T, gc.T
 
 
 def solution(mesh):

time: 41.3 us -> 35.9 us (0.87)
  local copies, waits for them, and re-layouts: 5.29 us -> 0 us
    pallas_call x2 -> x0, local copies, waits for them, and re-layouts: 2.06 us -> none  [on_device(): pl.pallas_call(functools.partial(unpack_kernel, tm, states), out_shape=[w...]
    reshape x2 -> x0, local copies, waits for them, and re-layouts: 1.82 us -> none  [the longest x1 1.26 us: on_device(): conv_bias.reshape(1, width)]
    unnamed x10 -> x0, local copies, waits for them, and re-layouts: 1.41 us -> none
where the time goes in v2:
time: 35.9 us; the launch traced here: 35.6 us
  Pallas kernels  35 us (97%)
  between operations  0.64 us (2%)
    pallas_call x1, Pallas kernels, on_device(): pl.pallas_call(functools.partial(kernel, tm, chan), out_shape=[jax.ShapeD...  33.1 us
    pallas_call x1, Pallas kernels, on_device(): pl.pallas_call(functools.partial(unpack_kernel, tm, states), out_shape=[w...  1.86 us

profile of v2, /device:TPU:0, one launch (start us, length us, event | category | flops | bytes accessed | tf_op | source)
XLA Modules:
  0.0 35.6 jit_solution(14759842368689073643)
XLA Ops:
  0.6 33.1 %shard_map.137 = (bf16[8,16,288]{2,1,0:T(8,128)(2,1)}, bf16[8,16,288]{2,1,0:T(8,128)(2,1)}) custom-call(bf16[64,288]{1,0:T(8,128)(2,1)} %x_ref.1, bf16[64,288]{1,0:T(8,128)(2,1)} %z_ref.1, bf16[64,288]{1,0:T(8,128)(2,1)} %dt_ref.1, bf16[64,288]{1,0:T(8,128)(2,1)} %g_ref.1, bf16[16,64]{1,0:T(8,128)(2,1)} %bitcast.4, bf16[16,64]{1,0:T(8,128)(2,1)} %bitcast.5, ...), custom_call_target="tpu_custom_call" | custom-call | tf_op jit(solution)/shard_map/pallas_call | solution.py:575
  33.8 1.9 %shard_map.138 = (bf16[64,288]{1,0:T(8,128)(2,1)}, bf16[64,288]{1,0:T(8,128)(2,1)}, bf16[64,288]{1,0:T(8,128)(2,1)}, bf16[16,64]{1,0:T(8,128)(2,1)}, bf16[16,64]{1,0:T(8,128)(2,1)}) custom-call(bf16[8,16,288]{2,1,0:T(8,128)(2,1)} %get-tuple-element.12.a_ref, bf16[8,16,288]{2,1,0:T(8,128)(2,1)} %get-tuple-element.13.b_ref), custom_call_target="tpu_custom_call" | custom-call | tf_op jit(solution)/shard_map/pallas_call | solution.py:598

commit v3 on v1

--- a/solution.py
+++ b/solution.py
@@ -21,6 +21,10 @@
 
 def dot(left, right):
     return jnp.dot(left, right, preferred_element_type=F32)
+
+
+def dot_t(left, right):
+    return lax.dot_general(left, right, (((1,), (1,)), ((), ())), preferred_element_type=F32)
 
 
 def iotas(shape):
@@ -75,6 +79,19 @@
 def kernel(
     tm,
     chan,
+    x_any,
+    z_any,
+    dt_any,
+    g_any,
+    b_any,
+    c_any,
+    w_any,
+    bias_any,
+    log_any,
+    skip_any,
+    out_a,
+    out_b,
+    out_p,
     x_ref,
     z_ref,
     dt_ref,
@@ -85,20 +102,19 @@
     bias_ref,
     log_ref,
     skip_ref,
-    out_a,
-    out_b,
     send_1,
     send_2,
     send_h,
     recv_1,
     recv_2,
     recv_h,
-    ends,
+    end_up,
+    end_down,
     ends_in,
+    tot,
+    tot_in,
     part,
-    part_in,
-    edge,
-    edge_in,
+    send_p,
     send_a,
     send_b,
     xpad,
@@ -117,66 +133,80 @@
     bc_s,
     fs_s,
     prod,
+    sem_in,
     sem_1,
     sem_2,
     sem_h,
     sem_e,
+    sem_t,
     sem_p,
-    sem_g,
     sem_a,
     sem_b,
 ):
     me = lax.axis_index("tm")
     ch = lax.axis_index("chan")
     length, width = x_ref.shape
-    states = b_ref.shape[1]
+    states = b_ref.shape[0]
     taps = w_ref.shape[0]
     frames = length // (S_DEV * tm)
     per = S_DEV * frames
     wide = width + 2 * states
     base = width // 128 * 128
 
-    def partner(k):
-        return lax.rem(me + k, tm)
-
-    def peer(k):
-        return lax.rem(ch + k, chan)
-
     def over_tm(body):
         def step(k, carry):
-            body(partner(k))
+            down = tm - 1 - k
+            down = jnp.where(down > me, down, down - 1)
+            up = jnp.where(k < me, k, k + 1)
+            body(jnp.where(me < tm // 2, down, up))
             return carry
 
-        lax.fori_loop(1, tm, step, 0)
-
-    def over_chan(body):
-        for k in range(1, chan):
-            body(peer(k))
+        lax.fori_loop(0, tm - 1, step, 0)
+
+    def over_all(body):
+        for j in range(chan):
+            c = lax.rem(ch + j, chan)
+
+            def step(k, carry):
+                body(lax.rem(me + k, tm), c)
+                return carry
+
+            lax.fori_loop(0 if j else 1, tm, step, 0)
 
     barrier = pltpu.get_barrier_semaphore()
 
-    def greet(d):
-        pl.semaphore_signal(barrier, inc=1, device_id={"tm": d}, device_id_type=MESH)
-
-    def greet_peer(d):
-        pl.semaphore_signal(barrier, inc=1, device_id={"chan": d}, device_id_type=MESH)
-
-    over_tm(greet)
-    over_chan(greet_peer)
+    def greet(d, c):
+        pl.semaphore_signal(
+            barrier, inc=1, device_id={"tm": d, "chan": c}, device_id_type=MESH
+        )
+
+    over_all(greet)
+    outside = (
+        x_any, z_any, dt_any, g_any, b_any, c_any, w_any, bias_any, log_any, skip_any
+    )
+    inside = (x_ref, z_ref, dt_ref, g_ref, b_ref, c_ref, w_ref, bias_ref, log_ref, skip_ref)
+    loads = [
+        pltpu.make_async_copy(source, target, sem_in.at[k])
+        for k, (source, target) in enumerate(zip(outside, inside))
+    ]
+    for load in loads:
+        load.start()
+    for load in loads:
+        load.wait()
 
     row, lane = iotas((width, wide))
     ex = ones_where(row == lane)
     row, lane = iotas((states, wide))
     eb = ones_where(lane == row + width)
     ec = ones_where(lane == row + width + states)
-    x_ext = (dot(x_ref[...], ex) + dot(b_ref[...], eb) + dot(c_ref[...], ec)).astype(BF16)
+    x_ext = dot(x_ref[...], ex).astype(BF16)
     first = pack_matrix(row_of, 0, tm, per, frames, length)
     second = pack_matrix(row_of, 1, tm, per, frames, length)
     dt_ext = dot(dt_ref[...], ex).astype(BF16)
-    one = (dot(first, x_ext) + dot(second, dt_ext)).astype(BF16)
-    two = (dot(first, z_ref[...]) + dot(second, g_ref[...])).astype(BF16)
-    send_1[...] = one.reshape(tm, 2 * per, wide)
-    send_2[...] = two.reshape(tm, 2 * per, width)
+    b_rows = dot_t(first, b_ref[...]).astype(BF16)
+    c_rows = dot_t(first, c_ref[...]).astype(BF16)
+    one = dot(first, x_ext) + dot(second, dt_ext) + dot(b_rows, eb) + dot(c_rows, ec)
+    send_1[...] = one.astype(BF16).reshape(tm, 2 * per, wide)
     packed, row = iotas((tm * 16, length))
     slot = packed & 15
     frame = slot - (8 - frames)
@@ -184,8 +214,6 @@
     good = (frame >= 0) & (slot < 8) & (packed >= 16)
     halo = ones_where(jnp.where(good, source, -1) == row)
     send_h[...] = dot(halo, x_ref[...]).astype(BF16).reshape(tm, 16, width)
-
-    pl.semaphore_wait(barrier, tm - 1 + chan - 1)
 
     def copy_tm(src, dst, sems, d, origin):
         return pltpu.make_async_remote_copy(
@@ -218,8 +246,11 @@
         def _():
             copy_h(d).start()
 
+    pl.semaphore_wait(barrier, tm * chan - 1)
     over_tm(start_halo)
     over_tm(lambda d: copy_1(d, me).start())
+    two = dot(first, z_ref[...]) + dot(second, g_ref[...])
+    send_2[...] = two.astype(BF16).reshape(tm, 2 * per, width)
     over_tm(lambda d: copy_2(d, me).start())
     recv_1[me] = send_1[me]
     recv_2[me] = send_2[me]
@@ -264,7 +295,7 @@
     dt_s[...] = dt_vals
     deltas = jnp.maximum(dt_vals, 0.0) + jnp.log(1.0 + jnp.exp(-jnp.abs(dt_vals)))
     delta_s[...] = deltas
-    pre = bias_ref[...] + w_ref[0:1, :] * xpad[8 - taps + 1 : 8 - taps + 1 + length, :]
+    pre = bias_ref[...].reshape(1, width) + w_ref[0:1, :] * xpad[8 - taps + 1 : 8 - taps + 1 + length, :]
     for k in range(1, taps):
         pre = pre + w_ref[k : k + 1, :] * xpad[8 - taps + 1 + k : 8 - taps + 1 + k + length, :]
     pre_s[...] = pre
@@ -272,6 +303,14 @@
     conv_s[...] = conv
     u_s[...] = deltas * conv
     total = jnp.sum(deltas, axis=0, keepdims=True)
+    padded = jnp.concatenate([total, jnp.zeros((1, 128 - width % 128), F32)], axis=1)
+    lines = [padded[:, k : k + 128] for k in range(0, width, 128)]
+    tot[...] = jnp.concatenate(lines + [jnp.zeros((8 - len(lines), 128), F32)], axis=0)
+
+    def copy_tot(d, origin):
+        return copy_tm(tot, tot_in.at[origin], sem_t, d, origin)
+
+    over_tm(lambda d: copy_tot(d, me).start())
 
     over_tm(lambda d: copy_2(d, d).wait_recv())
     got_2 = recv_2[...].reshape(tm * 2 * per, width)
@@ -305,18 +344,14 @@
         return state, back
 
     end, back_end = lax.fori_loop(0, length // 8, local, (zero, zero))
-    row = lax.broadcasted_iota(jnp.int32, (16, width), 0)
-    high = total.astype(BF16).astype(F32)
-    sums = jnp.where(row == 0, high, jnp.where(row == 1, total - high, 0.0))
-    ends[0:16, :] = end.astype(BF16)
-    ends[16:32, :] = sums.astype(BF16)
-    ends[32:48, :] = back_end.astype(BF16)
+    end_up[...] = end.astype(BF16)
+    end_down[...] = back_end.astype(BF16)
 
     def copy_up(d, origin):
-        return copy_tm(ends.at[0:32], ends_in.at[origin, 0:32], sem_e, d, origin)
+        return copy_tm(end_up, ends_in.at[origin], sem_e, d, origin)
 
     def copy_down(d, origin):
-        return copy_tm(ends.at[16:48], ends_in.at[origin, 16:48], sem_e, d, origin)
+        return copy_tm(end_down, ends_in.at[origin], sem_e, d, origin)
 
     def send_end(d):
         @pl.when(d > me)
@@ -330,17 +365,20 @@
     over_tm(send_end)
 
     def through(source):
-        pair = ends_in[source, 16:32, :].astype(F32)
-        return jnp.exp(rate * (pair[0:1] + pair[1:2]))
+        lines = tot_in[source]
+        pieces = [lines[k : k + 1, : min(128, width - 128 * k)] for k in range(-(-width // 128))]
+        return jnp.exp(rate * jnp.concatenate(pieces, axis=1))
+
+    over_tm(lambda d: copy_tot(d, d).wait_recv())
 
     def enter_up(source, state):
         copy_up(source, source).wait_recv()
-        return through(source) * state + ends_in[source, 0:16, :].astype(F32)
+        return through(source) * state + ends_in[source].astype(F32)
 
     def enter_down(turn, back):
         source = tm - 1 - turn
         copy_down(source, source).wait_recv()
-        return through(source) * back + ends_in[source, 32:48, :].astype(F32)
+        return through(source) * back + ends_in[source].astype(F32)
 
     state_in = lax.fori_loop(0, me, enter_up, zero)
     back_in = lax.fori_loop(0, tm - 1 - me, enter_down, zero)
@@ -349,7 +387,7 @@
     at_b = lane == (row & (states - 1))
     at_c = lane == (row & (states - 1)) + states
     ones = jnp.ones((width, 128), BF16)
-    skip = skip_ref[...]
+    skip = skip_ref[...].reshape(1, width)
 
     def picked(product, where):
         sums = jnp.where(where, dot(product, ones), 0.0)
@@ -392,38 +430,49 @@
 
     lax.fori_loop(0, length // BLK, backward, back_in)
 
-    def copy_part(d, origin):
+    def copy_a(d, origin):
+        return copy_tm(send_a.at[d], out_a.at[origin], sem_a, d, origin)
+
+    def copy_b(d, origin):
+        return copy_tm(send_b.at[d], out_b.at[origin], sem_b, d, origin)
+
+    def copy_p(d, c, from_d, from_c):
         return pltpu.make_async_remote_copy(
-            src_ref=part,
-            dst_ref=part_in.at[origin],
-            send_sem=sem_p.at[0, d],
-            recv_sem=sem_p.at[1, origin],
-            device_id={"chan": d},
+            src_ref=send_p.at[d],
+            dst_ref=out_p.at[from_c, from_d],
+            send_sem=sem_p.at[0, c, d],
+            recv_sem=sem_p.at[1, from_c, from_d],
+            device_id={"tm": d, "chan": c},
             device_id_type=MESH,
         )
 
-    over_chan(lambda d: copy_part(d, ch).start())
+    packed, row = iotas((tm * per, length))
+    place = ((packed & (per - 1)) >> log2(frames)) * (frames * tm)
+    place = place + (packed >> log2(per)) * frames + (packed & (frames - 1))
+    give = ones_where(place == row)
+    sums = part[...]
+    high = sums.astype(BF16)
+    low = (sums - high.astype(F32)).astype(BF16)
+    send_p[...] = (dot(give, high) + dot(give, low)).reshape(tm, per, 128)
+    over_all(lambda d, c: copy_p(d, c, me, ch).start())
+
     deltas = delta_s[...]
     weighted = w_s[...]
     grad_pre = (skip * dy_s[...] + deltas * weighted) * silu_grad(pre_s[...])
-    gp_s[0:length, :] = grad_pre
-    edge[...] = grad_pre[0:8]
-
-    def copy_edge(d):
-        return pltpu.make_async_remote_copy(
-            src_ref=edge,
-            dst_ref=edge_in,
-            send_sem=sem_g.at[0],
-            recv_sem=sem_g.at[1],
-            device_id={"tm": d},
-            device_id_type=MESH,
-        )
-
-    before = jnp.maximum(me - 1, 0)
-
-    @pl.when(me > 0)
-    def _():
-        copy_edge(before).start()
+    gp_s[0:8, :] = jnp.zeros((8, width), F32)
+    gp_s[8 : 8 + length, :] = grad_pre
+    gp_s[8 + length :, :] = jnp.zeros((8, width), F32)
+    grad_x = w_ref[0:1, :] * gp_s[taps - 1 : taps + 7 + length, :]
+    for k in range(1, taps):
+        grad_x = grad_x + w_ref[k : k + 1, :] * gp_s[taps - 1 - k : taps + 7 - k + length, :]
+    packed, row = iotas((tm * 2 * per, length + 8))
+    place = place_of(packed, 0, tm, per, frames)
+    slot = packed & (2 * per - 1)
+    spill = (packed >= (tm - 1) * 2 * per) & (slot > 2 * per - taps)
+    column = jnp.where(place >= 0, place + 8, jnp.where(spill, slot + 8 - 2 * per, -1))
+    both = dot(ones_where(column == row), grad_x.astype(BF16)).astype(BF16)
+    send_b[...] = both.reshape(tm, 2 * per, width)
+    over_tm(lambda d: copy_b(d, me).start())
 
     give_0 = pack_matrix(place_of, 0, tm, per, frames, length)
     give_1 = pack_matrix(place_of, 1, tm, per, frames, length)
@@ -432,38 +481,10 @@
     grad_z = (g_s[...] * seq_y * silu_grad(z_s[...])).astype(BF16)
     both = (dot(give_0, grad_dt) + dot(give_1, grad_z)).astype(BF16)
     send_a[...] = both.reshape(tm, 2 * per, width)
-
-    def copy_a(d, origin):
-        return copy_tm(send_a.at[d], out_a.at[origin], sem_a, d, origin)
-
-    def copy_b(d, origin):
-        return copy_tm(send_b.at[d], out_b.at[origin], sem_b, d, origin)
-
     over_tm(lambda d: copy_a(d, me).start())
+    out_p[ch, me] = send_p[me]
+    out_b[me] = send_b[me]
     out_a[me] = send_a[me]
-
-    @pl.when(me < tm - 1)
-    def _():
-        copy_edge(before).wait_recv()
-        gp_s[length:, :] = edge_in[...]
-
-    @pl.when(me == tm - 1)
-    def _():
-        gp_s[length:, :] = jnp.zeros((8, width), F32)
-
-    grad_x = w_ref[0:1, :] * gp_s[taps - 1 : taps - 1 + length, :]
-    for k in range(1, taps):
-        grad_x = grad_x + w_ref[k : k + 1, :] * gp_s[taps - 1 - k : taps - 1 - k + length, :]
-    x_part = dot(give_0, grad_x.astype(BF16))
-    over_chan(lambda d: copy_part(d, d).wait_recv())
-    part_in[ch] = part[...]
-    bc = part_in[0]
-    for k in range(1, chan):
-        bc = bc + part_in[k]
-    bc = jnp.concatenate([bc.astype(BF16), jnp.zeros((length, width - 128), BF16)], axis=1)
-    send_b[...] = (x_part + dot(give_1, bc)).astype(BF16).reshape(tm, 2 * per, width)
-    over_tm(lambda d: copy_b(d, me).start())
-    out_b[me] = send_b[me]
 
     over_tm(lambda d: copy_1(d, me).wait_send())
     over_tm(lambda d: copy_2(d, me).wait_send())
@@ -485,33 +506,44 @@
             copy_down(d, me).wait_send()
 
     over_tm(end_ends)
-    over_chan(lambda d: copy_part(d, ch).wait_send())
-
-    @pl.when(me > 0)
-    def _():
-        copy_edge(before).wait_send()
-
+    over_tm(lambda d: copy_tot(d, me).wait_send())
+    over_all(lambda d, c: copy_p(d, c, me, ch).wait_send())
     over_tm(lambda d: copy_a(d, me).wait_send())
     over_tm(lambda d: copy_b(d, me).wait_send())
     over_tm(lambda d: copy_a(d, d).wait_recv())
     over_tm(lambda d: copy_b(d, d).wait_recv())
-
-
-def unpack_kernel(tm, states, a_ref, b_ref, gx_ref, gdt_ref, gz_ref, gb_ref, gc_ref):
+    over_all(lambda d, c: copy_p(d, c, d, c).wait_recv())
+
+
+def unpack_kernel(tm, states, taps, a_ref, b_ref, p_ref, gx_ref, gdt_ref, gz_ref, gb_ref, gc_ref):
     length, width = gx_ref.shape
     frames = length // (S_DEV * tm)
     per = S_DEV * frames
     take_0 = unpack_matrix(row_of, 0, tm, per, frames, length)
     take_1 = unpack_matrix(row_of, 1, tm, per, frames, length)
+    row, packed = iotas((length, tm * 2 * per))
+    slot = packed & (2 * per - 1)
+    owner = (packed >> log2(2 * per)) - 1
+    frame = slot - 2 * per + frames
+    added = frame * (S_DEV * tm) + owner * S_DEV + S_DEV - 1
+    added = jnp.where((slot > 2 * per - taps) & (owner >= 0), added, -1)
+    both = ones_where((row_of(packed, 0, tm, per, frames) == row) | (added == row))
     got_a = a_ref[...].reshape(tm * 2 * per, width)
     got_b = b_ref[...].reshape(tm * 2 * per, width)
     gdt_ref[...] = dot(take_0, got_a).astype(BF16)
     gz_ref[...] = dot(take_1, got_a).astype(BF16)
-    gx_ref[...] = dot(take_0, got_b).astype(BF16)
-    bc = dot(take_1, got_b[:, 0:128]).astype(BF16)
-    row, lane = iotas((128, states))
-    gb_ref[...] = dot(bc, ones_where(row == lane)).astype(BF16)
-    gc_ref[...] = dot(bc, ones_where(row == lane + states)).astype(BF16)
+    gx_ref[...] = dot(both, got_b).astype(BF16)
+    sums = p_ref[0]
+    for k in range(1, p_ref.shape[0]):
+        sums = sums + p_ref[k]
+    row, packed = iotas((length, tm * per))
+    source = (packed & (frames - 1)) * (S_DEV * tm) + (packed >> log2(per)) * S_DEV
+    source = source + ((packed & (per - 1)) >> log2(frames))
+    thin = sums.reshape(tm * per, 128).astype(BF16)
+    bc = dot(ones_where(source == row), thin).astype(BF16)
+    row, lane = iotas((states, 128))
+    gb_ref[...] = dot_t(ones_where(row == lane), bc).astype(BF16)
+    gc_ref[...] = dot_t(ones_where(row + states == lane), bc).astype(BF16)
 
 
 def on_device(
@@ -531,72 +563,82 @@
     length, width = inner_x.shape
     states = input_b.shape[1]
     per = length // tm
+    assert per % 8 == 0 and length // (S_DEV * tm) >= conv_weight.shape[0] - 1
     wide = width + 2 * states
     vmem = pl.BlockSpec(memory_space=pltpu.VMEM)
     rows = pltpu.VMEM((length, width), F32)
     block = (tm, 2 * per, width)
     sems = pltpu.SemaphoreType.DMA
     limit = 60 * 1024 * 1024
+    arrays = (
+        inner_x,
+        gate_z,
+        dt_raw,
+        grad_out,
+        input_b.T,
+        output_c.T,
+        conv_weight,
+        conv_bias,
+        decay_log,
+        skip_gain,
+    )
     scratch = [
+        *[pltpu.VMEM(array.shape, array.dtype) for array in arrays],
         pltpu.VMEM((tm, 2 * per, wide), BF16),
         pltpu.VMEM(block, BF16),
         pltpu.VMEM((tm, 16, width), BF16),
         pltpu.VMEM((tm, 2 * per, wide), BF16),
         pltpu.VMEM(block, BF16),
         pltpu.VMEM((16, width), BF16),
-        pltpu.VMEM((48, width), BF16),
-        pltpu.VMEM((tm, 48, width), BF16),
+        pltpu.VMEM((16, width), BF16),
+        pltpu.VMEM((16, width), BF16),
+        pltpu.VMEM((tm, 16, width), BF16),
+        pltpu.VMEM((8, 128), F32),
+        pltpu.VMEM((tm, 8, 128), F32),
         pltpu.VMEM((length, 128), F32),
-        pltpu.VMEM((chan, length, 128), F32),
-        pltpu.VMEM((8, width), F32),
-        pltpu.VMEM((8, width), F32),
+        pltpu.VMEM((tm, per, 128), F32),
         pltpu.VMEM(block, BF16),
         pltpu.VMEM(block, BF16),
         pltpu.VMEM((length + 8, width), F32),
         *[rows] * 11,
-        pltpu.VMEM((length + 8, width), F32),
+        pltpu.VMEM((length + 16, width), F32),
         pltpu.VMEM((length * states, 256), F32),
         pltpu.VMEM((length * states, width), F32),
         pltpu.VMEM((3, BLK * states, width), BF16),
+        sems((10,)),
         sems((2, tm)),
         sems((2, tm)),
         sems((tm + 1,)),
         sems((2, tm)),
-        sems((2, chan)),
-        sems((2,)),
+        sems((2, tm)),
+        sems((2, chan, tm)),
         sems((2, tm)),
         sems((2, tm)),
     ]
-    out_a, out_b = pl.pallas_call(
+    out_a, out_b, out_p = pl.pallas_call(
         functools.partial(kernel, tm, chan),
-        out_shape=[jax.ShapeDtypeStruct(block, BF16)] * 2,
-        in_specs=[vmem] * 10,
-        out_specs=[vmem] * 2,
+        out_shape=[
+            jax.ShapeDtypeStruct(block, BF16),
+            jax.ShapeDtypeStruct(block, BF16),
+            jax.ShapeDtypeStruct((chan, tm, per, 128), F32),
+        ],
+        in_specs=[pl.BlockSpec(memory_space=pl.ANY)] * 10,
+        out_specs=[vmem] * 3,
         scratch_shapes=scratch,
         compiler_params=pltpu.CompilerParams(
             collective_id=0, has_side_effects=True, vmem_limit_bytes=limit
         ),
-    )(
-        inner_x,
-        gate_z,
-        dt_raw,
-        grad_out,
-        input_b,
-        output_c,
-        conv_weight,
-        conv_bias.reshape(1, width),
-        decay_log,
-        skip_gain.reshape(1, width),
-    )
+    )(*arrays)
     wide_out = jax.ShapeDtypeStruct((length, width), BF16)
-    thin_out = jax.ShapeDtypeStruct((length, states), BF16)
-    return pl.pallas_call(
-        functools.partial(unpack_kernel, tm, states),
+    thin_out = jax.ShapeDtypeStruct((states, length), BF16)
+    gx, gdt, gz, gb, gc = pl.pallas_call(
+        functools.partial(unpack_kernel, tm, states, conv_weight.shape[0]),
         out_shape=[wide_out, wide_out, wide_out, thin_out, thin_out],
-        in_specs=[vmem] * 2,
+        in_specs=[vmem] * 3,
         out_specs=[vmem] * 5,
         compiler_params=pltpu.CompilerParams(vmem_limit_bytes=limit),
-    )(out_a, out_b)
+    )(out_a, out_b, out_p)
+    return gx, gdt, gz, gb.T, gc.T
 
 
 def solution(mesh):

time: 41.3 us -> 37 us (0.90)
  local copies, waits for them, and re-layouts: 5.29 us -> 0 us
  Pallas kernels: 35 us -> 36.1 us
    pallas_call x2 -> x0, local copies, waits for them, and re-layouts: 2.06 us -> none  [on_device(): pl.pallas_call(functools.partial(unpack_kernel, tm, states), out_shape=[w...]
    reshape x2 -> x0, local copies, waits for them, and re-layouts: 1.82 us -> none  [the longest x1 1.26 us: on_device(): conv_bias.reshape(1, width)]
    unnamed x10 -> x0, local copies, waits for them, and re-layouts: 1.41 us -> none
    pallas_call x1, Pallas kernels: 33.2 us -> 34.2 us  [on_device(): pl.pallas_call(functools.partial(kernel, tm, chan), out_shape=[jax.ShapeD...]
where the time goes in v3:
time: 37 us; the launch traced here: 36.8 us
  Pallas kernels  36.1 us (98%)
  between operations  0.64 us (2%)
    pallas_call x1, Pallas kernels, on_device(): pl.pallas_call(functools.partial(kernel, tm, chan), out_shape=[jax.ShapeD...  34.2 us
    pallas_call x1, Pallas kernels, on_device(): pl.pallas_call(functools.partial(unpack_kernel, tm, states, conv_weight.s...  1.92 us

profile of v3, /device:TPU:0, one launch (start us, length us, event | category | flops | bytes accessed | tf_op | source)
XLA Modules:
  0.0 36.8 jit_solution(6428634678903404943)
XLA Ops:
  0.6 34.2 %shard_map.137 = (bf16[8,16,288]{2,1,0:T(8,128)(2,1)}, bf16[8,16,288]{2,1,0:T(8,128)(2,1)}, f32[4,8,8,128]{3,2,1,0:T(8,128)}) custom-call(bf16[64,288]{1,0:T(8,128)(2,1)} %x_any.1, bf16[64,288]{1,0:T(8,128)(2,1)} %z_any.1, bf16[64,288]{1,0:T(8,128)(2,1)} %dt_any.1, bf16[64,288]{1,0:T(8,128)(2,1)} %g_any.1, bf16[16,64]{1,0:T(8,128)(2,1)} %bitcast.4, ...), custom_call_target="tpu_custom_call" | custom-call | tf_op jit(solution)/shard_map/pallas_call | solution.py:618
  34.9 1.9 %shard_map.138 = (bf16[64,288]{1,0:T(8,128)(2,1)}, bf16[64,288]{1,0:T(8,128)(2,1)}, bf16[64,288]{1,0:T(8,128)(2,1)}, bf16[16,64]{1,0:T(8,128)(2,1)}, bf16[16,64]{1,0:T(8,128)(2,1)}) custom-call(bf16[8,16,288]{2,1,0:T(8,128)(2,1)} %get-tuple-element.13.a_ref, bf16[8,16,288]{2,1,0:T(8,128)(2,1)} %get-tuple-element.14.b_ref, ...), custom_call_target="tpu_custom_call" | custom-call | tf_op jit(solution)/shard_map/pallas_call | solution.py:634

commit v4 on v3

--- a/solution.py
+++ b/solution.py
@@ -114,6 +114,7 @@
     tot,
     tot_in,
     part,
+    part_in,
     send_p,
     send_a,
     send_b,
@@ -140,6 +141,7 @@
     sem_e,
     sem_t,
     sem_p,
+    sem_c,
     sem_a,
     sem_b,
 ):
@@ -155,23 +157,14 @@
 
     def over_tm(body):
         def step(k, carry):
-            down = tm - 1 - k
-            down = jnp.where(down > me, down, down - 1)
-            up = jnp.where(k < me, k, k + 1)
-            body(jnp.where(me < tm // 2, down, up))
+            body(lax.rem(me + k + 1, tm))
             return carry
 
         lax.fori_loop(0, tm - 1, step, 0)
 
-    def over_all(body):
-        for j in range(chan):
-            c = lax.rem(ch + j, chan)
-
-            def step(k, carry):
-                body(lax.rem(me + k, tm), c)
-                return carry
-
-            lax.fori_loop(0 if j else 1, tm, step, 0)
+    def over_chan(body):
+        for j in range(1, chan):
+            body(lax.rem(ch + j, chan))
 
     barrier = pltpu.get_barrier_semaphore()
 
@@ -180,7 +173,8 @@
             barrier, inc=1, device_id={"tm": d, "chan": c}, device_id_type=MESH
         )
 
-    over_all(greet)
+    over_tm(lambda d: greet(d, ch))
+    over_chan(lambda c: greet(me, c))
     outside = (
         x_any, z_any, dt_any, g_any, b_any, c_any, w_any, bias_any, log_any, skip_any
     )
@@ -246,7 +240,7 @@
         def _():
             copy_h(d).start()
 
-    pl.semaphore_wait(barrier, tm * chan - 1)
+    pl.semaphore_wait(barrier, tm + chan - 2)
     over_tm(start_halo)
     over_tm(lambda d: copy_1(d, me).start())
     two = dot(first, z_ref[...]) + dot(second, g_ref[...])
@@ -436,25 +430,20 @@
     def copy_b(d, origin):
         return copy_tm(send_b.at[d], out_b.at[origin], sem_b, d, origin)
 
-    def copy_p(d, c, from_d, from_c):
+    def copy_p(d, origin):
+        return copy_tm(send_p.at[d], out_p.at[0, origin], sem_p, d, origin)
+
+    def copy_part(c, origin):
         return pltpu.make_async_remote_copy(
-            src_ref=send_p.at[d],
-            dst_ref=out_p.at[from_c, from_d],
-            send_sem=sem_p.at[0, c, d],
-            recv_sem=sem_p.at[1, from_c, from_d],
-            device_id={"tm": d, "chan": c},
+            src_ref=part,
+            dst_ref=part_in.at[origin],
+            send_sem=sem_c.at[0, c],
+            recv_sem=sem_c.at[1, origin],
+            device_id={"chan": c},
             device_id_type=MESH,
         )
 
-    packed, row = iotas((tm * per, length))
-    place = ((packed & (per - 1)) >> log2(frames)) * (frames * tm)
-    place = place + (packed >> log2(per)) * frames + (packed & (frames - 1))
-    give = ones_where(place == row)
-    sums = part[...]
-    high = sums.astype(BF16)
-    low = (sums - high.astype(F32)).astype(BF16)
-    send_p[...] = (dot(give, high) + dot(give, low)).reshape(tm, per, 128)
-    over_all(lambda d, c: copy_p(d, c, me, ch).start())
+    over_chan(lambda c: copy_part(c, ch).start())
 
     deltas = delta_s[...]
     weighted = w_s[...]
@@ -482,7 +471,20 @@
     both = (dot(give_0, grad_dt) + dot(give_1, grad_z)).astype(BF16)
     send_a[...] = both.reshape(tm, 2 * per, width)
     over_tm(lambda d: copy_a(d, me).start())
-    out_p[ch, me] = send_p[me]
+    packed, row = iotas((tm * per, length))
+    place = ((packed & (per - 1)) >> log2(frames)) * (frames * tm)
+    place = place + (packed >> log2(per)) * frames + (packed & (frames - 1))
+    give = ones_where(place == row)
+    over_chan(lambda c: copy_part(c, c).wait_recv())
+    part_in[ch] = part[...]
+    sums = part_in[0]
+    for k in range(1, chan):
+        sums = sums + part_in[k]
+    high = sums.astype(BF16)
+    low = (sums - high.astype(F32)).astype(BF16)
+    send_p[...] = (dot(give, high) + dot(give, low)).reshape(tm, per, 128)
+    over_tm(lambda d: copy_p(d, me).start())
+    out_p[0, me] = send_p[me]
     out_b[me] = send_b[me]
     out_a[me] = send_a[me]
 
@@ -507,12 +509,13 @@
 
     over_tm(end_ends)
     over_tm(lambda d: copy_tot(d, me).wait_send())
-    over_all(lambda d, c: copy_p(d, c, me, ch).wait_send())
+    over_tm(lambda d: copy_p(d, me).wait_send())
+    over_chan(lambda c: copy_part(c, ch).wait_send())
     over_tm(lambda d: copy_a(d, me).wait_send())
     over_tm(lambda d: copy_b(d, me).wait_send())
     over_tm(lambda d: copy_a(d, d).wait_recv())
     over_tm(lambda d: copy_b(d, d).wait_recv())
-    over_all(lambda d, c: copy_p(d, c, d, c).wait_recv())
+    over_tm(lambda d: copy_p(d, d).wait_recv())
 
 
 def unpack_kernel(tm, states, taps, a_ref, b_ref, p_ref, gx_ref, gdt_ref, gz_ref, gb_ref, gc_ref):
@@ -596,6 +599,7 @@
         pltpu.VMEM((8, 128), F32),
         pltpu.VMEM((tm, 8, 128), F32),
         pltpu.VMEM((length, 128), F32),
+        pltpu.VMEM((chan, length, 128), F32),
         pltpu.VMEM((tm, per, 128), F32),
         pltpu.VMEM(block, BF16),
         pltpu.VMEM(block, BF16),
@@ -611,7 +615,8 @@
         sems((tm + 1,)),
         sems((2, tm)),
         sems((2, tm)),
-        sems((2, chan, tm)),
+        sems((2, tm)),
+        sems((2, chan)),
         sems((2, tm)),
         sems((2, tm)),
     ]
@@ -620,7 +625,7 @@
         out_shape=[
             jax.ShapeDtypeStruct(block, BF16),
             jax.ShapeDtypeStruct(block, BF16),
-            jax.ShapeDtypeStruct((chan, tm, per, 128), F32),
+            jax.ShapeDtypeStruct((1, tm, per, 128), F32),
         ],
         in_specs=[pl.BlockSpec(memory_space=pl.ANY)] * 10,
         out_specs=[vmem] * 3,

time: 37 us -> 34.2 us (0.924)
  Pallas kernels: 36.1 us -> 33.3 us
    pallas_call x1, Pallas kernels: 34.2 us -> 31.5 us  [on_device(): pl.pallas_call(functools.partial(kernel, tm, chan), out_shape=[jax.ShapeD...]
where the time goes in v4:
time: 34.2 us; the launch traced here: 34 us
  Pallas kernels  33.3 us (97%)
  between operations  0.64 us (2%)
    pallas_call x1, Pallas kernels, on_device(): pl.pallas_call(functools.partial(kernel, tm, chan), out_shape=[jax.ShapeD...  31.5 us
    pallas_call x1, Pallas kernels, on_device(): pl.pallas_call(functools.partial(unpack_kernel, tm, states, conv_weight.s...  1.86 us

profile of v4, /device:TPU:0, one launch (start us, length us, event | category | flops | bytes accessed | tf_op | source)
XLA Modules:
  0.0 34.0 jit_solution(10328903029989048974)
XLA Ops:
  0.6 31.5 %shard_map.137 = (bf16[8,16,288]{2,1,0:T(8,128)(2,1)}, bf16[8,16,288]{2,1,0:T(8,128)(2,1)}, f32[1,8,8,128]{3,2,1,0:T(8,128)}) custom-call(bf16[64,288]{1,0:T(8,128)(2,1)} %x_any.1, bf16[64,288]{1,0:T(8,128)(2,1)} %z_any.1, bf16[64,288]{1,0:T(8,128)(2,1)} %dt_any.1, bf16[64,288]{1,0:T(8,128)(2,1)} %g_any.1, bf16[16,64]{1,0:T(8,128)(2,1)} %bitcast.4, ...), custom_call_target="tpu_custom_call" | custom-call | tf_op jit(solution)/shard_map/pallas_call | solution.py:623
  32.1 1.9 %shard_map.138 = (bf16[64,288]{1,0:T(8,128)(2,1)}, bf16[64,288]{1,0:T(8,128)(2,1)}, bf16[64,288]{1,0:T(8,128)(2,1)}, bf16[16,64]{1,0:T(8,128)(2,1)}, bf16[16,64]{1,0:T(8,128)(2,1)}) custom-call(bf16[8,16,288]{2,1,0:T(8,128)(2,1)} %get-tuple-element.13.a_ref, bf16[8,16,288]{2,1,0:T(8,128)(2,1)} %get-tuple-element.14.b_ref, ...), custom_call_target="tpu_custom_call" | custom-call | tf_op jit(solution)/shard_map/pallas_call | solution.py:639
